TPU v7x, 32 devices: a whole 2x2x4 slice. The times are simulated.
32 devices in a mesh: comp: 2 (over y), gy: 4 (over z), gx: 4 (over x, core).
Axes of the slice: x: 2, y: 2, z: 4, core: 2. Of those that a mesh axis runs over, the one named last changes fastest.
Arguments:
- spectra: float32 [32, 36, 16, 512], P('comp', None, 'gy', 'gx'), may hold values from 0.05 to 2
- wind_field: float32 [2, 16, 512], P(None, 'gy', 'gx'), may hold values from -5 to 5
- sea_mask: int32 [16, 512], P('gy', 'gx'), may hold values 0 or 1
- first_layer: bfloat16 [1152, 1024], replicated, may hold values from -0.1875 to 0.1875
- second_layer: bfloat16 [1024, 1152], replicated, may hold values from -0.1875 to 0.1875
- ocean_state: float32 [4, 16, 16, 512], P(None, None, 'gy', 'gx'), may hold values from -4 to 4
- current_blocks: float32 [16, 2, 512, 128], P('gy', None, 'gx'), may hold values from 0 to 1
- current_rows: int32 [16, 2, 4], P('gy', None, 'gx'), may hold values from 0 to 15, as said below
- stress_blocks: float32 [16, 2, 512, 128], P('gy', None, 'gx'), may hold values from 0 to 1
- stress_rows: int32 [16, 2, 4], P('gy', None, 'gx'), may hold values from 0 to 15, as said below
Outputs:
- spectra_next: float32 [32, 36, 16, 512], P('comp', None, 'gy', 'gx')
- ocean_next: float32 [4, 16, 16, 512], P(None, None, 'gy', 'gx')
Inputs may be any that keep to these rules, and one draw needn't show every extreme that they name: `current_rows`: entry [r, b, t] is the source row read by block b of destination row r in column tile t; it lies within one row of r, and both r - 1 and r + 1 occur. `stress_rows`: entry [r, b, t] is the source row read by block b of destination row r in column tile t; it lies within one row of r, and both r - 1 and r + 1 occur.
All inputs are finite; a program needn't handle non-finite values. No bound on the sum of `sea_mask` on one device may be relied on, other than what follows from the above.
Results may differ from a plain program's by a relative error of at most 0.0023.
Values may be sent and summed in bfloat16 or wider, within the bound.
A program may use at most 64 MiB of HBM per device.

v0:
```python
import jax
import jax.numpy as jnp
from jax import lax
from jax.sharding import PartitionSpec as P

STEPS = 2


CURRENT_GAIN = 0.08
WIND_GAIN = 0.06
DECAY_GAIN = 0.03
NONLINEAR_GAIN = 0.3
THERMAL = 0.2
HALINE = 0.8
CORIOLIS = 0.1
PRESSURE_GAIN = 0.2
LATERAL_MIX = 0.1
VERTICAL_MIX = 0.2
ADVECTION = 0.3
STRESS_GAIN = 150.0


def padded_2(cells, sides, width):
    for axis, dim in sides:
        count = lax.axis_size(axis)
        ends = count - 1
        head = lax.slice_in_dim(cells, 0, width, axis=dim)
        tail = lax.slice_in_dim(cells, cells.shape[dim] - width, cells.shape[dim], axis=dim)
        cells = jnp.concatenate(
            [
                lax.ppermute(tail, axis, [(i, (i + 1) % count) for i in range(ends)]),
                cells,
                lax.ppermute(head, axis, [((i + 1) % count, i) for i in range(ends)]),
            ],
            axis=dim,
        )
    return cells


def partner_2(shard, axis, distance):
    return lax.ppermute(shard, axis, [(i, i ^ 1 << distance) for i in range(lax.axis_size(axis))])


def spectral_tables(first, count, total, directions):
    freq_index = (jnp.arange(count) + first).astype(jnp.float32)
    group_speed = 0.4 * jnp.exp(-3.0 * freq_index / (total - 1))
    phase_speed = 4.0 * group_speed
    freq_ratio = jnp.exp(2.0 * freq_index / (total - 1) - 1.0)
    angles = 2.0 * jnp.pi * jnp.arange(directions).astype(jnp.float32) / directions
    return (group_speed, phase_speed, freq_ratio, jnp.cos(angles), jnp.sin(angles))


def advect(spectrum, padded, group_speed, cosines, sines, currents, mask_f):
    western = padded[:, :, 1:-1, :-2]
    eastern = padded[:, :, 1:-1, 2:]
    southern = padded[:, :, :-2, 1:-1]
    northern = padded[:, :, 2:, 1:-1]
    speed_x = (
        group_speed[:, None, None, None] * cosines[None, :, None, None] + CURRENT_GAIN * currents[0]
    )
    speed_y = (
        group_speed[:, None, None, None] * sines[None, :, None, None] + CURRENT_GAIN * currents[1]
    )
    flux_sum = jnp.maximum(speed_x, 0.0) * (spectrum - western) + jnp.minimum(speed_x, 0.0) * (
        eastern - spectrum
    )
    flux_sum = (
        flux_sum
        + jnp.maximum(speed_y, 0.0) * (spectrum - southern)
        + jnp.minimum(speed_y, 0.0) * (northern - spectrum)
    )
    return mask_f * (spectrum - flux_sum)


def source_rates(propagated, wind_field, phase_speed, freq_ratio, cosines, sines):
    growth = WIND_GAIN * jnp.maximum(
        wind_field[0] * cosines[None, :, None, None]
        + wind_field[1] * sines[None, :, None, None]
        - phase_speed[:, None, None, None],
        0.0,
    )
    energy = jnp.sum(propagated, axis=(0, 1))
    moment = jnp.sum(freq_ratio[:, None, None, None] * propagated, axis=(0, 1))
    push_x = jnp.sum(growth * propagated * cosines[None, :, None, None], axis=(0, 1))
    push_y = jnp.sum(growth * propagated * sines[None, :, None, None], axis=(0, 1))
    return (growth, (energy, moment, push_x, push_y))


def contract(left, right):
    return lax.dot_general(
        left, right, (((0,), (0,)), ((), ())), preferred_element_type=jnp.float32
    )


def ocean_update(padded, stress, mask_f):

    def middle(field):
        return field[..., 1:-1, 1:-1]

    def eastern(field):
        return field[..., 1:-1, 2:]

    def western(field):
        return field[..., 1:-1, :-2]

    def northern(field):
        return field[..., 2:, 1:-1]

    def southern(field):
        return field[..., :-2, 1:-1]

    def spread(field):
        return (
            eastern(field)
            + western(field)
            + northern(field)
            + southern(field)
            - 4.0 * middle(field)
        )

    def column(field):
        upper_level = jnp.concatenate([field[:1], field[:-1]], axis=0)
        lower_level = jnp.concatenate([field[1:], field[-1:]], axis=0)
        return upper_level + lower_level - 2.0 * field

    density = -THERMAL * padded[2] + HALINE * padded[3]
    pressure = jnp.cumsum(density, axis=0) - 0.5 * density
    speed_u = middle(padded[0])
    speed_v = middle(padded[1])

    def carry_term(field):
        return speed_u * 0.5 * (eastern(field) - western(field)) + speed_v * 0.5 * (
            northern(field) - southern(field)
        )

    surface = (jnp.arange(padded.shape[1]) == 0).astype(jnp.float32)[:, None, None]
    tend_u = (
        CORIOLIS * speed_v
        - PRESSURE_GAIN * 0.5 * (eastern(pressure) - western(pressure))
        + LATERAL_MIX * spread(padded[0])
        + VERTICAL_MIX * column(speed_u)
        + STRESS_GAIN * surface * stress[0]
    )
    tend_v = (
        -CORIOLIS * speed_u
        - PRESSURE_GAIN * 0.5 * (northern(pressure) - southern(pressure))
        + LATERAL_MIX * spread(padded[1])
        + VERTICAL_MIX * column(speed_v)
        + STRESS_GAIN * surface * stress[1]
    )
    tend_t = (
        -ADVECTION * carry_term(padded[2])
        + LATERAL_MIX * spread(padded[2])
        + VERTICAL_MIX * column(middle(padded[2]))
    )
    tend_s = (
        -ADVECTION * carry_term(padded[3])
        + LATERAL_MIX * spread(padded[3])
        + VERTICAL_MIX * column(middle(padded[3]))
    )
    return middle(padded) + mask_f * jnp.stack([tend_u, tend_v, tend_t, tend_s])


def neighbour_rows(field):
    return padded_2(field, (("gy", 1),), 1)


def regrid(padded_rows, blocks, row_table, row_count):
    first_row = lax.axis_index("gy") * row_count
    local_rows = row_table[:, :, 0] - first_row + 1
    selected = jnp.take(padded_rows, local_rows, axis=1)
    return jnp.einsum("rbds,krbs->krd", blocks, selected, precision=lax.Precision.HIGHEST)


def local(
    spectra,
    wind_field,
    sea_mask,
    first_layer,
    second_layer,
    ocean_state,
    current_blocks,
    current_rows,
    stress_blocks,
    stress_rows,
):
    mask_f = sea_mask.astype(jnp.float32)
    row_count, col_count = sea_mask.shape
    half_freqs, directions = (spectra.shape[0], spectra.shape[1])
    freq_total = half_freqs * lax.axis_size("comp")
    comp_total = freq_total * directions
    comp_index = lax.axis_index("comp")
    group_speed, phase_speed, freq_ratio, cosines, sines = spectral_tables(
        comp_index * half_freqs, half_freqs, freq_total, directions
    )
    levels = ocean_state.shape[1]
    flat_ocean = ocean_state.reshape(4 * levels, row_count, col_count)
    source_field = neighbour_rows(jnp.stack([ocean_state[0, 0], ocean_state[1, 0]]))
    currents = regrid(source_field, current_blocks, current_rows, row_count)
    spectrum = spectra
    stress_sum = jnp.zeros((2, row_count, col_count), jnp.float32)
    for step_index in range(STEPS):
        padded = padded_2(spectrum, (("gy", 2), ("gx", 3)), 1)
        propagated = advect(spectrum, padded, group_speed, cosines, sines, currents, mask_f)
        growth, partials = source_rates(
            propagated, wind_field, phase_speed, freq_ratio, cosines, sines
        )
        energy, moment, push_x, push_y = lax.psum(
            (partials[0], partials[1], partials[2], partials[3]), "comp"
        )
        energy_floor = jnp.maximum(energy, 1.0)
        scaled = (propagated * (comp_total / energy_floor)).astype(jnp.bfloat16)
        partner = partner_2(scaled, "comp", 0)
        is_low = comp_index == 0
        low_half = jnp.where(is_low, scaled, partner)
        high_half = jnp.where(is_low, partner, scaled)
        complete = jnp.concatenate([low_half, high_half], axis=0).reshape(
            comp_total, row_count * col_count
        )
        hidden = jax.nn.silu(contract(first_layer, complete)).astype(jnp.bfloat16)
        own_rows = lax.dynamic_slice_in_dim(
            second_layer, comp_index * half_freqs * directions, half_freqs * directions, 1
        )
        transfer = (
            contract(own_rows, hidden)
            .astype(jnp.bfloat16)
            .reshape(half_freqs, directions, row_count, col_count)
        )
        damping = DECAY_GAIN * freq_ratio[:, None, None, None] * (moment / energy_floor) ** 2
        spectrum = propagated * jnp.exp(growth - damping) + NONLINEAR_GAIN * (
            energy_floor / comp_total
        ) * transfer.astype(jnp.float32)
        stress_sum = stress_sum + jnp.stack([push_x, push_y]) / comp_total
    stress = stress_sum / STEPS
    joined = jnp.concatenate([flat_ocean, stress], axis=0)
    joined_padded = padded_2(joined, (("gy", 1), ("gx", 2)), 1)
    stress_ocean = regrid(
        joined_padded[4 * levels :, :, 1:-1], stress_blocks, stress_rows, row_count
    )
    padded_ocean = joined_padded[: 4 * levels].reshape(4, levels, row_count + 2, col_count + 2)
    ocean_next = ocean_update(padded_ocean, stress_ocean, mask_f)
    return (spectrum, ocean_next)


def solution(mesh):
    placed = (
        P("comp", None, "gy", "gx"),
        P(None, "gy", "gx"),
        P("gy", "gx"),
        P(),
        P(),
        P(None, None, "gy", "gx"),
        P("gy", None, "gx", None),
        P("gy", None, "gx"),
        P("gy", None, "gx", None),
        P("gy", None, "gx"),
    )
    return jax.shard_map(
        local,
        mesh=mesh,
        in_specs=placed,
        out_specs=(P("comp", None, "gy", "gx"), P(None, None, "gy", "gx")),
        check_vma=False,
    )
```

profile of v0, /device:TPU:0, one launch (start us, length us, event | category | flops | bytes accessed | tf_op | source)
XLA Modules:
  0.0 246.2 jit_solution(151973454647523252)
XLA Ops:
  5.0 6.3 %collective-permute-start.2 = (f32[16,36,1,128]{3,0,2,1:T(8,128)}, f32[16,36,1,128]{3,0,2,1:T(8,128)}, u32[]{:S(2)}, u32[]{:S(2)}) collective-permute-start(f32[16,36,1,128]{3,0,2,1:T(8,128)} %copy.194), channel_id=1, source_target_pairs={{0,4},{4,8},{8,12},{1,5},{5,9},{9,13},{2,6},{6,10},{10,14},{3,7},{... | collective-permute-start | bytes 884744 | tf_op jit(solution)/shard_map/ppermute | solution.py:31
  14.0 4.5 %collective-permute-start = (f32[2,1,128]{2,0,1:T(2,128)S(1)}, f32[2,1,128]{2,0,1:T(2,128)S(1)}, u32[]{:S(2)}, u32[]{:S(2)}) collective-permute-start(f32[2,1,128]{2,0,1:T(2,128)S(1)} %get-tuple-element.69), channel_id=1, source_target_pairs={{0,4},{4,8},{8,12},{1,5},{5,9},{9,13},{2,6},{6,10},{10,14},{3,7},{... | collective-permute-start | bytes 3080 | tf_op jit(solution)/shard_map/ppermute | solution.py:31
  22.3 3.7 %copy.169 = f32[16,36,4,128]{1,0,3,2:T(8,128)} copy(f32[16,36,4,128]{3,2,1,0:T(4,128)} %param.12) | data formatting | bytes 2359296 | tf_op args[0]
  33.6 3.0 %collective-permute-start.4 = (f32[16,36,6,1]{1,0,3,2:T(8,128)S(1)}, f32[16,36,6,1]{1,0,3,2:T(8,128)S(1)}, u32[]{:S(2)}, u32[]{:S(2)}) collective-permute-start(f32[16,36,6,1]{1,0,3,2:T(8,128)S(1)} %get-tuple-element.33), channel_id=1, source_target_pairs={{0,1},{1,2},{2,3},{4,5},{5,6},{6,7},{8,9},{9,10},{10,11},{12,13},{... | collective-permute-start | bytes 41480 | tf_op jit(solution)/shard_map/ppermute | solution.py:31
  37.6 16.6 %multiply_reduce_fusion.3 = (f32[4,128]{1,0:T(4,128)}, f32[4,128]{1,0:T(4,128)}, f32[4,128]{1,0:T(4,128)S(1)}, f32[4,128]{1,0:T(4,128)S(1)}, f32[16,36,4,128]{1,0,3,2:T(8,128)}) fusion(f32[36]{0:T(128)S(1)} %get-tuple-element.84, f32[16]{0:T(128)S(1)} %broadcast_multiply_fusion.5, f32[36,4,128]{0,2,1:T(8,128)S(1)} %copy-done.5, f32[36]{0:T(128)S(1)} %get-tuple-element.83, ...), kind=kLoop, calls=%fused_computation.53 | loop fusion | flops 11204608 | bytes 3069856 | tf_op jit(solution)/shard_map/reduce_sum | solution.py:84
  54.2 5.1 %all-reduce.1 = (f32[4,128]{1,0:T(4,128)S(1)}, f32[4,128]{1,0:T(4,128)S(1)}) all-reduce(f32[4,128]{1,0:T(4,128)S(1)} %get-tuple-element.19, f32[4,128]{1,0:T(4,128)S(1)} %get-tuple-element.20), channel_id=1, replica_groups=mesh['comp'=2,'gy'=4,'gx'=4] {'comp'}, use_global_device_ids=true, to_apply=%region_3.5 | all-reduce | flops 1024 | bytes 8192 | tf_op jit(solution)/shard_map/psum | solution.py:208
  59.3 3.6 %multiply_convert_fusion.1 = bf16[16,36,4,128]{1,0,3,2:T(8,128)(2,1)} fusion(f32[16,36,4,128]{1,0,3,2:T(8,128)} %get-tuple-element.30, f32[4,128]{1,0:T(4,128)S(1)} %get-tuple-element.78), kind=kLoop, calls=%fused_computation.58 | loop fusion | flops 589824 | bytes 1771520 | tf_op jit(solution)/shard_map/convert_element_type | solution.py:212
  62.9 4.1 %copy.170 = bf16[16,36,4,128]{3,0,2,1:T(8,128)(2,1)} copy(bf16[16,36,4,128]{1,0,3,2:T(8,128)(2,1)} %multiply_convert_fusion.1) | data formatting | bytes 1179648 | tf_op jit(solution)/shard_map/convert_element_type | solution.py:212
  71.0 12.2 %collective-permute-done.6 = bf16[16,36,4,128]{3,0,2,1:T(8,128)(2,1)} collective-permute-done((bf16[16,36,4,128]{3,0,2,1:T(8,128)(2,1)}, bf16[16,36,4,128]{3,0,2,1:T(8,128)(2,1)}, u32[]{:S(2)}, u32[]{:S(2)}) %collective-permute-start.6) | collective-permute-done | bytes 589856 | tf_op jit(solution)/shard_map/ppermute | solution.py:41
  83.3 3.8 %copy.171 = bf16[16,36,4,128]{1,0,3,2:T(8,128)(2,1)} copy(bf16[16,36,4,128]{3,0,2,1:T(8,128)(2,1)} %collective-permute-done.6) | data formatting | bytes 1179648 | tf_op jit(solution)/shard_map/ppermute | solution.py:41
  87.1 3.2 %broadcast_select_fusion.3 = (bf16[16,36,4,128]{1,0,3,2:T(8,128)(2,1)S(1)}, bf16[16,36,4,128]{1,0,3,2:T(8,128)(2,1)S(1)}) fusion(bf16[16,36,4,128]{1,0,3,2:T(8,128)(2,1)} %copy.171, pred[]{:T(512)S(6)} %eq.13, f32[16,36,4,128]{1,0,3,2:T(8,128)} %get-tuple-element.30, f32[4,128]{1,0:T(4,128)S(1)} %get-tuple-element.78), kind=kLoop, calls=%fused_computation.78 | loop fusion | flops 1179648 | bytes 2951169 | tf_op jit(solution)/shard_map/jit(_where)/select_n | solution.py:215
  90.4 2.8 %pad_maximum_fusion.16 = bf16[32,36,4,128]{1,0,3,2:T(8,128)(2,1)} fusion(bf16[16,36,4,128]{1,0,3,2:T(8,128)(2,1)S(1)} %get-tuple-element.40, bf16[16,36,4,128]{1,0,3,2:T(8,128)(2,1)S(1)} %get-tuple-element.39), kind=kLoop, calls=%fused_computation.48 | loop fusion | flops 2359296 | bytes 2359296 | tf_op jit(solution)/shard_map/concatenate | solution.py:217
  93.2 8.6 %reshape.241 = bf16[1152,512]{0,1:T(8,128)(2,1)} reshape(bf16[32,36,4,128]{1,0,3,2:T(8,128)(2,1)} %pad_maximum_fusion.16) | data formatting | bytes 2359296 | tf_op jit(solution)/shard_map/reshape | solution.py:217
  101.8 5.0 %fusion.37 = f32[576,512]{1,0:T(8,128)} fusion(bf16[1152,512]{0,1:T(8,128)(2,1)} %reshape.241, bf16[1152,1024]{1,0:T(8,128)(2,1)S(1)} %copy-done, bf16[1024,1152]{1,0:T(8,128)(2,1)} %param.16, s32[]{:T(128)S(6)} %select_n.31), kind=kOutput, calls=%fused_computation.82 | convolution fusion | flops 1815150592 | bytes 6029316 | tf_op jit(solution)/shard_map/dot_general | solution.py:90
  109.5 3.7 %copy.174 = f32[16,36,4,128]{1,0,3,2:T(8,128)} copy(f32[16,36,4,128]{3,2,1,0:T(4,128)} %reshape.209) | data formatting | bytes 2359296 | tf_op jit(solution)/shard_map/convert_element_type | solution.py:232
  113.2 4.9 %multiply_add_fusion.1 = f32[16,36,4,128]{1,0,3,2:T(8,128)S(1)} fusion(f32[16,36,4,128]{1,0,3,2:T(8,128)} %copy.174, f32[16,36,4,128]{1,0,3,2:T(8,128)} %get-tuple-element.30, f32[4,128]{1,0:T(4,128)S(1)} %get-tuple-element.77, f32[16,4,128]{0,2,1:T(8,128)S(1)} %broadcast_multiply_fusion.1, f32[16]{0:T(128)S(1)} %broadcast_multiply_fusion.5, ...), kind=kLoop, calls=%fused_computation.57 | loop fusion | flops 2064384 | bytes 3647552 | tf_op jit(solution)/shard_map/add | solution.py:230
  126.1 5.3 %collective-permute-start.7 = (f32[16,36,1,128]{3,0,2,1:T(8,128)}, f32[16,36,1,128]{3,0,2,1:T(8,128)}, u32[]{:S(2)}, u32[]{:S(2)}) collective-permute-start(f32[16,36,1,128]{3,0,2,1:T(8,128)} %copy.175), channel_id=1, source_target_pairs={{0,4},{4,8},{8,12},{1,5},{5,9},{9,13},{2,6},{6,10},{10,14},{3,7},{... | collective-permute-start | bytes 884744 | tf_op jit(solution)/shard_map/ppermute | solution.py:31
  142.1 3.7 %collective-permute-start.9 = (f32[16,36,6,1]{1,0,3,2:T(8,128)}, f32[16,36,6,1]{1,0,3,2:T(8,128)}, u32[]{:S(2)}, u32[]{:S(2)}) collective-permute-start(f32[16,36,6,1]{1,0,3,2:T(8,128)} %get-tuple-element.31), channel_id=1, source_target_pairs={{0,1},{1,2},{2,3},{4,5},{5,6},{6,7},{8,9},{9,10},{10,11},{12,13},{... | collective-permute-start | bytes 41480 | tf_op jit(solution)/shard_map/ppermute | solution.py:31
  147.6 19.3 %multiply_reduce_fusion.1 = (f32[4,128]{1,0:T(4,128)}, f32[4,128]{1,0:T(4,128)}, f32[4,128]{1,0:T(4,128)}, f32[4,128]{1,0:T(4,128)}, f32[16,36,4,128]{1,0,3,2:T(8,128)}) fusion(f32[36]{0:T(128)} %copy-done.27, f32[16]{0:T(128)} %copy-done.24, f32[36,4,128]{0,2,1:T(8,128)} %multiply_add_fusion.2, f32[36]{0:T(128)} %copy-done.26, f32[16]{0:T(128)} %get-tuple-element.81, ...), kind=kLoop, calls=%fused_computation.51 | loop fusion | flops 11204608 | bytes 3069856 | tf_op jit(solution)/shard_map/reduce_sum | solution.py:84
  166.9 8.3 %all-reduce = (f32[4,128]{1,0:T(4,128)S(1)}, f32[4,128]{1,0:T(4,128)S(1)}, f32[1,4,128]{2,1,0:T(4,128)S(1)}, f32[1,4,128]{2,1,0:T(4,128)S(1)}, f32[1,4,128]{2,1,0:T(4,128)S(1)}, /*index=5*/f32[1,4,128]{2,1,0:T(4,128)S(1)}) all-reduce(f32[4,128]{1,0:T(4,128)} %get-tuple-element.17, ...), channel_id=1, replica_groups=mesh['comp'=2,'gy'=4,'gx'=4] {'comp'}, use_global_device_ids=true, to_apply=%region_7.9 | all-reduce | flops 3072 | bytes 24576 | tf_op jit(solution)/shard_map/psum | solution.py:208
  176.4 3.6 %multiply_convert_fusion = bf16[16,36,4,128]{1,0,3,2:T(8,128)(2,1)} fusion(f32[16,36,4,128]{1,0,3,2:T(8,128)} %get-tuple-element.29, f32[4,128]{1,0:T(4,128)S(1)} %get-tuple-element.75), kind=kLoop, calls=%fused_computation.55 | loop fusion | flops 589824 | bytes 1771520 | tf_op jit(solution)/shard_map/convert_element_type | solution.py:212
  180.0 4.1 %copy.181 = bf16[16,36,4,128]{3,0,2,1:T(8,128)(2,1)} copy(bf16[16,36,4,128]{1,0,3,2:T(8,128)(2,1)} %multiply_convert_fusion) | data formatting | bytes 1179648 | tf_op jit(solution)/shard_map/convert_element_type | solution.py:212
  186.4 5.0 %collective-permute-start.12 = (f32[66,1,128]{2,1,0:T(1,128)S(1)}, f32[66,1,128]{2,1,0:T(1,128)S(1)}, u32[]{:S(2)}, u32[]{:S(2)}) collective-permute-start(f32[66,1,128]{2,1,0:T(1,128)S(1)} %get-tuple-element.45), channel_id=1, source_target_pairs={{0,4},{4,8},{8,12},{1,5},{5,9},{9,13},{2,6},{6,10},{10,14},{3,7},{... | collective-permute-start | bytes 101384 | tf_op jit(solution)/shard_map/ppermute | solution.py:31
  195.2 3.0 %collective-permute-start.14 = (f32[66,6,1]{2,1,0:T(8,128)S(1)}, f32[66,6,1]{2,1,0:T(8,128)S(1)}, u32[]{:S(2)}, u32[]{:S(2)}) collective-permute-start(f32[66,6,1]{2,1,0:T(8,128)S(1)} %get-tuple-element.43), channel_id=1, source_target_pairs={{0,1},{1,2},{2,3},{4,5},{5,6},{6,7},{8,9},{9,10},{10,11},{12,13},{... | collective-permute-start | bytes 4760 | tf_op jit(solution)/shard_map/ppermute | solution.py:31
  207.0 3.8 %copy.182 = bf16[16,36,4,128]{1,0,3,2:T(8,128)(2,1)} copy(bf16[16,36,4,128]{3,0,2,1:T(8,128)(2,1)} %collective-permute-done.11) | data formatting | bytes 1179648 | tf_op jit(solution)/shard_map/ppermute | solution.py:41
  210.8 3.2 %broadcast_select_fusion.1 = (bf16[16,36,4,128]{1,0,3,2:T(8,128)(2,1)S(1)}, bf16[16,36,4,128]{1,0,3,2:T(8,128)(2,1)S(1)}) fusion(bf16[16,36,4,128]{1,0,3,2:T(8,128)(2,1)} %copy.182, pred[]{:T(512)S(6)} %eq.13, f32[16,36,4,128]{1,0,3,2:T(8,128)} %get-tuple-element.29, f32[4,128]{1,0:T(4,128)S(1)} %copy-done.21), kind=kLoop, calls=%fused_computation.76 | loop fusion | flops 1179648 | bytes 2951169 | tf_op jit(solution)/shard_map/jit(_where)/select_n | solution.py:215
  214.1 2.8 %pad_maximum_fusion.17 = bf16[32,36,4,128]{1,0,3,2:T(8,128)(2,1)} fusion(bf16[16,36,4,128]{1,0,3,2:T(8,128)(2,1)S(1)} %get-tuple-element.36, bf16[16,36,4,128]{1,0,3,2:T(8,128)(2,1)S(1)} %get-tuple-element.35), kind=kLoop, calls=%fused_computation.49 | loop fusion | flops 2359296 | bytes 2359296 | tf_op jit(solution)/shard_map/concatenate | solution.py:217
  216.9 7.9 %reshape.242 = bf16[1152,512]{0,1:T(8,128)(2,1)S(1)} reshape(bf16[32,36,4,128]{1,0,3,2:T(8,128)(2,1)} %pad_maximum_fusion.17) | data formatting | bytes 2359296 | tf_op jit(solution)/shard_map/reshape | solution.py:217
  224.8 4.7 %fusion.36 = f32[576,512]{1,0:T(8,128)} fusion(bf16[1152,512]{0,1:T(8,128)(2,1)S(1)} %reshape.242, bf16[1152,1024]{1,0:T(8,128)(2,1)S(1)} %copy-done, bf16[1024,1152]{1,0:T(8,128)(2,1)} %param.16, s32[]{:T(128)S(6)} %select_n.31), kind=kOutput, calls=%fused_computation.80 | convolution fusion | flops 1815150592 | bytes 6029316 | tf_op jit(solution)/shard_map/dot_general | solution.py:90
  232.1 3.7 %copy.185 = f32[16,36,4,128]{1,0,3,2:T(8,128)} copy(f32[16,36,4,128]{3,2,1,0:T(4,128)} %reshape.210) | data formatting | bytes 2359296 | tf_op jit(solution)/shard_map/convert_element_type | solution.py:232
  235.9 6.6 %multiply_add_fusion = f32[16,36,4,128]{1,0,3,2:T(8,128)} fusion(f32[16,36,4,128]{1,0,3,2:T(8,128)} %copy.185, f32[16,36,4,128]{1,0,3,2:T(8,128)} %get-tuple-element.29, f32[4,128]{1,0:T(4,128)S(1)} %copy-done.28, f32[16,4,128]{0,2,1:T(8,128)S(1)} %copy-done.8, f32[16]{0:T(128)S(1)} %copy-done.25, f32[36,4,128]{0,2,1:T(8,128)S(1)} %copy-done.7), kind=kLoop, calls=%fused_computation.54 | loop fusion | flops 2064384 | bytes 3647552 | tf_op jit(solution)/shard_map/add | solution.py:230
  242.5 3.7 %copy.189 = f32[16,36,4,128]{3,2,1,0:T(4,128)} copy(f32[16,36,4,128]{1,0,3,2:T(8,128)} %multiply_add_fusion) | data formatting | bytes 2359296
  (159 shorter events, 64.7 us)
Async XLA Ops:
  0.6 101.2 %copy-start = (bf16[1152,1024]{1,0:T(8,128)(2,1)S(1)}, bf16[1152,1024]{1,0:T(8,128)(2,1)}, u32[]{:S(2)}) copy-start(bf16[1152,1024]{1,0:T(8,128)(2,1)} %param.15) | copy-start | bytes 7077892
  0.6 25.5 %copy-start.34 = (s32[4,128]{1,0:T(4,128)S(1)}, s32[4,128]{1,0:T(4,128)}, u32[]{:S(2)}) copy-start(s32[4,128]{1,0:T(4,128)} %param.14) | copy-start | bytes 6148
  0.7 26.1 %copy-start.9 = (f32[4,2,128,128]{3,2,1,0:T(8,128)S(1)}, f32[4,2,128,128]{3,2,1,0:T(8,128)}, u32[]{:S(2)}) copy-start(f32[4,2,128,128]{3,2,1,0:T(8,128)} %param.18) | copy-start | bytes 1572868
  3.0 24.3 %collective-permute-start.3 = (f32[16,36,1,128]{3,0,2,1:T(8,128)S(1)}, f32[16,36,1,128]{3,0,2,1:T(8,128)}, u32[]{:S(2)}, u32[]{:S(2)}) collective-permute-start(f32[16,36,1,128]{3,0,2,1:T(8,128)S(1)} %copy.195), channel_id=1, source_target_pairs={{4,0},{8,4},{12,8},{5,1},{9,5},{13,9},{6,2},{10,6},{14,10},{7,3},{... | collective-permute-start | bytes 884744 | tf_op jit(solution)/shard_map/ppermute | solution.py:33
  5.0 23.8 %collective-permute-start.2 = (f32[16,36,1,128]{3,0,2,1:T(8,128)}, f32[16,36,1,128]{3,0,2,1:T(8,128)}, u32[]{:S(2)}, u32[]{:S(2)}) collective-permute-start(f32[16,36,1,128]{3,0,2,1:T(8,128)} %copy.194), channel_id=1, source_target_pairs={{0,4},{4,8},{8,12},{1,5},{5,9},{9,13},{2,6},{6,10},{10,14},{3,7},{... | collective-permute-start | bytes 884744 | tf_op jit(solution)/shard_map/ppermute | solution.py:31
  12.7 13.5 %collective-permute-start.1 = (f32[2,1,128]{2,0,1:T(2,128)S(1)}, f32[2,1,128]{2,0,1:T(2,128)S(1)}, u32[]{:S(2)}, u32[]{:S(2)}) collective-permute-start(f32[2,1,128]{2,0,1:T(2,128)S(1)} %get-tuple-element.70), channel_id=1, source_target_pairs={{4,0},{8,4},{12,8},{5,1},{9,5},{13,9},{6,2},{10,6},{14,10},{7,3},{... | collective-permute-start | bytes 3080 | tf_op jit(solution)/shard_map/ppermute | solution.py:33
  14.0 12.2 %collective-permute-start = (f32[2,1,128]{2,0,1:T(2,128)S(1)}, f32[2,1,128]{2,0,1:T(2,128)S(1)}, u32[]{:S(2)}, u32[]{:S(2)}) collective-permute-start(f32[2,1,128]{2,0,1:T(2,128)S(1)} %get-tuple-element.69), channel_id=1, source_target_pairs={{0,4},{4,8},{8,12},{1,5},{5,9},{9,13},{2,6},{6,10},{10,14},{3,7},{... | collective-permute-start | bytes 3080 | tf_op jit(solution)/shard_map/ppermute | solution.py:31
  18.6 19.0 %copy-start.26 = (f32[36]{0:T(128)}, f32[36]{0:T(128)S(1)}, u32[]{:S(2)}) copy-start(f32[36]{0:T(128)S(1)} %get-tuple-element.83) | copy-start | bytes 436
  18.6 19.0 %copy-start.27 = (f32[36]{0:T(128)}, f32[36]{0:T(128)S(1)}, u32[]{:S(2)}) copy-start(f32[36]{0:T(128)S(1)} %get-tuple-element.84) | copy-start | bytes 436
  22.3 90.9 %copy-start.24 = (f32[16]{0:T(128)}, f32[16]{0:T(128)S(1)}, u32[]{:S(2)}) copy-start(f32[16]{0:T(128)S(1)} %broadcast_multiply_fusion.5) | copy-start | bytes 196
  26.1 11.4 %copy-start.18 = (f32[4,128]{1,0:T(4,128)}, f32[4,128]{1,0:T(4,128)S(1)}, u32[]{:S(2)}) copy-start(f32[4,128]{1,0:T(4,128)S(1)} %convert_element_type.74) | copy-start | bytes 6148
  32.2 4.5 %collective-permute-start.5 = (f32[16,36,6,1]{1,0,3,2:T(8,128)S(1)}, f32[16,36,6,1]{1,0,3,2:T(8,128)S(1)}, u32[]{:S(2)}, u32[]{:S(2)}) collective-permute-start(f32[16,36,6,1]{1,0,3,2:T(8,128)S(1)} %get-tuple-element.34), channel_id=1, source_target_pairs={{1,0},{2,1},{3,2},{5,4},{6,5},{7,6},{9,8},{10,9},{11,10},{13,12},{... | collective-permute-start | bytes 41480 | tf_op jit(solution)/shard_map/ppermute | solution.py:33
  33.6 3.9 %collective-permute-start.4 = (f32[16,36,6,1]{1,0,3,2:T(8,128)S(1)}, f32[16,36,6,1]{1,0,3,2:T(8,128)S(1)}, u32[]{:S(2)}, u32[]{:S(2)}) collective-permute-start(f32[16,36,6,1]{1,0,3,2:T(8,128)S(1)} %get-tuple-element.33), channel_id=1, source_target_pairs={{0,1},{1,2},{2,3},{4,5},{5,6},{6,7},{8,9},{9,10},{10,11},{12,13},{... | collective-permute-start | bytes 41480 | tf_op jit(solution)/shard_map/ppermute | solution.py:31
  36.7 17.5 %copy-start.22 = (f32[1,4,128]{2,0,1:T(1,128)}, f32[1,4,128]{2,0,1:T(1,128)S(1)}, u32[]{:S(2)}) copy-start(f32[1,4,128]{2,0,1:T(1,128)S(1)} %get-tuple-element.67) | copy-start | bytes 6148
  36.7 17.5 %copy-start.23 = (f32[1,4,128]{2,0,1:T(1,128)}, f32[1,4,128]{2,0,1:T(1,128)S(1)}, u32[]{:S(2)}) copy-start(f32[1,4,128]{2,0,1:T(1,128)S(1)} %get-tuple-element.68) | copy-start | bytes 6148
  67.0 16.2 %collective-permute-start.6 = (bf16[16,36,4,128]{3,0,2,1:T(8,128)(2,1)}, bf16[16,36,4,128]{3,0,2,1:T(8,128)(2,1)}, u32[]{:S(2)}, u32[]{:S(2)}) collective-permute-start(bf16[16,36,4,128]{3,0,2,1:T(8,128)(2,1)} %copy.170), channel_id=1, source_target_pairs={{0,16},{16,0},{1,17},{17,1},{2,18},{18,2},{3,19},{19,3},{4,20},{20... | collective-permute-start | bytes 1769480 | tf_op jit(solution)/shard_map/ppermute | solution.py:41
  70.3 20.1 %copy-start.32 = (f32[16]{0:T(128)}, f32[16]{0:T(128)S(1)}, u32[]{:S(2)}) copy-start(f32[16]{0:T(128)S(1)} %broadcast_multiply_fusion.4) | copy-start | bytes 196
  123.6 10.9 %collective-permute-start.8 = (f32[16,36,1,128]{3,0,2,1:T(8,128)}, f32[16,36,1,128]{3,0,2,1:T(8,128)}, u32[]{:S(2)}, u32[]{:S(2)}) collective-permute-start(f32[16,36,1,128]{3,0,2,1:T(8,128)} %copy.176), channel_id=1, source_target_pairs={{4,0},{8,4},{12,8},{5,1},{9,5},{13,9},{6,2},{10,6},{14,10},{7,3},{... | collective-permute-start | bytes 884744 | tf_op jit(solution)/shard_map/ppermute | solution.py:33
  126.1 10.8 %collective-permute-start.7 = (f32[16,36,1,128]{3,0,2,1:T(8,128)}, f32[16,36,1,128]{3,0,2,1:T(8,128)}, u32[]{:S(2)}, u32[]{:S(2)}) collective-permute-start(f32[16,36,1,128]{3,0,2,1:T(8,128)} %copy.175), channel_id=1, source_target_pairs={{0,4},{4,8},{8,12},{1,5},{5,9},{9,13},{2,6},{6,10},{10,14},{3,7},{... | collective-permute-start | bytes 884744 | tf_op jit(solution)/shard_map/ppermute | solution.py:31
  140.8 6.8 %collective-permute-start.10 = (f32[16,36,6,1]{1,0,3,2:T(8,128)}, f32[16,36,6,1]{1,0,3,2:T(8,128)}, u32[]{:S(2)}, u32[]{:S(2)}) collective-permute-start(f32[16,36,6,1]{1,0,3,2:T(8,128)} %get-tuple-element.32), channel_id=1, source_target_pairs={{1,0},{2,1},{3,2},{5,4},{6,5},{7,6},{9,8},{10,9},{11,10},{13,12},{... | collective-permute-start | bytes 41480 | tf_op jit(solution)/shard_map/ppermute | solution.py:33
  142.1 5.5 %collective-permute-start.9 = (f32[16,36,6,1]{1,0,3,2:T(8,128)}, f32[16,36,6,1]{1,0,3,2:T(8,128)}, u32[]{:S(2)}, u32[]{:S(2)}) collective-permute-start(f32[16,36,6,1]{1,0,3,2:T(8,128)} %get-tuple-element.31), channel_id=1, source_target_pairs={{0,1},{1,2},{2,3},{4,5},{5,6},{6,7},{8,9},{9,10},{10,11},{12,13},{... | collective-permute-start | bytes 41480 | tf_op jit(solution)/shard_map/ppermute | solution.py:31
  176.4 15.0 %copy-start.33 = (f32[16]{0:T(128)S(1)}, f32[16]{0:T(128)}, u32[]{:S(2)}) copy-start(f32[16]{0:T(128)} %copy-done.32) | copy-start | bytes 196
  184.1 19.3 %copy-start.14 = (f32[15,4,128]{2,1,0:T(4,128)S(1)}, f32[15,4,128]{2,1,0:T(4,128)}, u32[]{:S(2)}) copy-start(f32[15,4,128]{2,1,0:T(4,128)} %get-tuple-element.52) | copy-start | bytes 92164
  184.1 22.9 %collective-permute-start.11 = (bf16[16,36,4,128]{3,0,2,1:T(8,128)(2,1)}, bf16[16,36,4,128]{3,0,2,1:T(8,128)(2,1)}, u32[]{:S(2)}, u32[]{:S(2)}) collective-permute-start(bf16[16,36,4,128]{3,0,2,1:T(8,128)(2,1)} %copy.181), channel_id=1, source_target_pairs={{0,16},{16,0},{1,17},{17,1},{2,18},{18,2},{3,19},{19,3},{4,20},{20... | collective-permute-start | bytes 1769480 | tf_op jit(solution)/shard_map/ppermute | solution.py:41
  185.1 7.2 %collective-permute-start.13 = (f32[66,1,128]{2,1,0:T(1,128)S(1)}, f32[66,1,128]{2,1,0:T(1,128)S(1)}, u32[]{:S(2)}, u32[]{:S(2)}) collective-permute-start(f32[66,1,128]{2,1,0:T(1,128)S(1)} %get-tuple-element.46), channel_id=1, source_target_pairs={{4,0},{8,4},{12,8},{5,1},{9,5},{13,9},{6,2},{10,6},{14,10},{7,3},{... | collective-permute-start | bytes 101384 | tf_op jit(solution)/shard_map/ppermute | solution.py:33
  186.4 6.6 %collective-permute-start.12 = (f32[66,1,128]{2,1,0:T(1,128)S(1)}, f32[66,1,128]{2,1,0:T(1,128)S(1)}, u32[]{:S(2)}, u32[]{:S(2)}) collective-permute-start(f32[66,1,128]{2,1,0:T(1,128)S(1)} %get-tuple-element.45), channel_id=1, source_target_pairs={{0,4},{4,8},{8,12},{1,5},{5,9},{9,13},{2,6},{6,10},{10,14},{3,7},{... | collective-permute-start | bytes 101384 | tf_op jit(solution)/shard_map/ppermute | solution.py:31
  191.4 12.9 %copy-start.12 = (f32[15,4,128]{2,1,0:T(4,128)S(1)}, f32[15,4,128]{2,1,0:T(4,128)}, u32[]{:S(2)}) copy-start(f32[15,4,128]{2,1,0:T(4,128)} %get-tuple-element.50) | copy-start | bytes 92164
  191.5 12.9 %copy-start.13 = (f32[15,4,128]{2,1,0:T(4,128)S(1)}, f32[15,4,128]{2,1,0:T(4,128)}, u32[]{:S(2)}) copy-start(f32[15,4,128]{2,1,0:T(4,128)} %get-tuple-element.51) | copy-start | bytes 92164
  193.1 12.1 %copy-start.10 = (f32[15,4,128]{2,1,0:T(4,128)S(1)}, f32[15,4,128]{2,1,0:T(4,128)}, u32[]{:S(2)}) copy-start(f32[15,4,128]{2,1,0:T(4,128)} %get-tuple-element.47) | copy-start | bytes 92164
  193.1 12.1 %copy-start.11 = (f32[15,4,128]{2,1,0:T(4,128)S(1)}, f32[15,4,128]{2,1,0:T(4,128)}, u32[]{:S(2)}) copy-start(f32[15,4,128]{2,1,0:T(4,128)} %get-tuple-element.54) | copy-start | bytes 92164
  193.9 7.3 %collective-permute-start.15 = (f32[66,6,1]{2,1,0:T(8,128)}, f32[66,6,1]{2,1,0:T(8,128)S(1)}, u32[]{:S(2)}, u32[]{:S(2)}) collective-permute-start(f32[66,6,1]{2,1,0:T(8,128)} %get-tuple-element.44), channel_id=1, source_target_pairs={{1,0},{2,1},{3,2},{5,4},{6,5},{7,6},{9,8},{10,9},{11,10},{13,12},{... | collective-permute-start | bytes 4760 | tf_op jit(solution)/shard_map/ppermute | solution.py:33
  195.2 6.0 %collective-permute-start.14 = (f32[66,6,1]{2,1,0:T(8,128)S(1)}, f32[66,6,1]{2,1,0:T(8,128)S(1)}, u32[]{:S(2)}, u32[]{:S(2)}) collective-permute-start(f32[66,6,1]{2,1,0:T(8,128)S(1)} %get-tuple-element.43), channel_id=1, source_target_pairs={{0,1},{1,2},{2,3},{4,5},{5,6},{6,7},{8,9},{9,10},{10,11},{12,13},{... | collective-permute-start | bytes 4760 | tf_op jit(solution)/shard_map/ppermute | solution.py:31
  (19 other events, 117.7 us)
where the time goes:
time: 249 us; the launch traced here: 246 us
  other arithmetic  81.6 us (33%)
  local copies, waits for them, and re-layouts  79.2 us (32%)
  starting transfers between devices  42.9 us (17%)
  waiting for transfers between devices  15.9 us (6%)
  blocking collectives  13.4 us (5%)
  matrix products  11.9 us (5%)
    reduce_sum x2, other arithmetic, source_rates(): jnp.sum(growth * propagated * cosines[None, :, None, None], axis=(0, 1))  35.9 us
    ppermute x7, starting transfers between devices, padded_2(): lax.ppermute(tail, axis, [(i, (i + 1) % count) for i in range(ends)])  30.8 us
    reshape x2, local copies, waits for them, and re-layouts, local(): jnp.concatenate([low_half, high_half], axis=0)  16.5 us
    psum x2, blocking collectives, local(): lax.psum((partials[0], partials[1], partials[2], partials[3]), 'comp')  13.4 us
    convert_element_type x4, local copies, waits for them, and re-layouts, local(): transfer.astype(jnp.float32)  12.8 us
    ppermute x2, waiting for transfers between devices, partner_2(): lax.ppermute(shard, axis, [(i, i ^ 1 << distance) for i in range(lax.axis...  12.2 us
    add x2, other arithmetic, local(): propagated * jnp.exp(growth - damping)  11.5 us
    unnamed x74, local copies, waits for them, and re-layouts  10.9 us
  transfers between devices with their start and end apart: 16, of which 5 were waited for; matrix products, arithmetic and copies ran while one was open for 13% of the time, Pallas kernels for 0%

commit v1 on v0

v1 whole, which is shorter than its diff:
```python
import numpy as np

import jax
import jax.numpy as jnp
from jax import lax
from jax.experimental import pallas as pl
from jax.experimental.pallas import tpu as pltpu
from jax.sharding import PartitionSpec as P

STEPS = 2


CURRENT_GAIN = 0.08
WIND_GAIN = 0.06
DECAY_GAIN = 0.03
NONLINEAR_GAIN = 0.3
THERMAL = 0.2
HALINE = 0.8
CORIOLIS = 0.1
PRESSURE_GAIN = 0.2
LATERAL_MIX = 0.1
VERTICAL_MIX = 0.2
ADVECTION = 0.3
STRESS_GAIN = 150.0


def from_lower(block, axis):
    count = lax.axis_size(axis)
    return lax.ppermute(block, axis, [(i, i + 1) for i in range(count - 1)])


def from_upper(block, axis):
    count = lax.axis_size(axis)
    return lax.ppermute(block, axis, [(i + 1, i) for i in range(count - 1)])


def partner_of(block):
    return lax.ppermute(block, "comp", [(0, 1), (1, 0)])


def tables(total, directions):
    index = np.arange(total, dtype=np.float64)
    group = 0.4 * np.exp(-3.0 * index / (total - 1))
    ratio = np.exp(2.0 * index / (total - 1) - 1.0)
    angles = 2.0 * np.pi * np.arange(directions) / directions
    cosines, sines = np.cos(angles), np.sin(angles)
    full = np.zeros((total, directions, 8))
    full[..., 0] = group[:, None] * cosines
    full[..., 1] = group[:, None] * sines
    full[..., 2] = cosines
    full[..., 3] = sines
    full[..., 4] = 4.0 * group[:, None]
    full[..., 5] = ratio[:, None]
    return full.reshape(total * directions, 8).astype(np.float32)


VMEM_LIMIT = 56 * 1024 * 1024
CHUNK = 48


def call(kernel, outs, scratch=(), flops=0, moved=0):
    return pl.pallas_call(
        kernel,
        out_shape=outs,
        scratch_shapes=list(scratch),
        compiler_params=pltpu.CompilerParams(vmem_limit_bytes=VMEM_LIMIT),
        cost_estimate=pl.CostEstimate(flops=flops, bytes_accessed=moved, transcendentals=0),
    )


def edges_kernel(state, low, high, ends):
    rows = state.shape[1]
    low[...] = state[:, 0, :].astype(jnp.bfloat16)
    high[...] = state[:, rows - 1, :].astype(jnp.bfloat16)
    for r in range(rows):
        values = state[:, r, :]
        ends[:, r : r + 1] = values[:, :1]
        ends[:, rows + r : rows + r + 1] = values[:, -1:]


def advect_kernel(state, south, north, west, east, table, currents, wind, mask, prop, prop_16, sums):
    comps, rows, cols = state.shape
    lane = lax.broadcasted_iota(jnp.int32, (CHUNK, cols), 1)

    def body(i, totals):
        part = pl.ds(pl.multiple_of(i * CHUNK, CHUNK), CHUNK)
        tab = table[part, :]
        gx, gy, cos, sin, phase, ratio = (
            jnp.broadcast_to(tab[:, n : n + 1], (CHUNK, cols)) for n in range(6)
        )
        near_w = west[part, :]
        near_e = east[part, :]
        lines = [south[part, :].astype(jnp.float32)]
        lines += [state[part, r, :] for r in range(rows)]
        lines += [north[part, :].astype(jnp.float32)]
        out = []
        for r in range(rows):
            here = lines[r + 1]
            before = jnp.where(lane == 0, near_w[:, r : r + 1], pltpu.roll(here, 1, 1))
            after = jnp.where(lane == cols - 1, near_e[:, r : r + 1], pltpu.roll(here, cols - 1, 1))
            cx = gx + CURRENT_GAIN * currents[0, r : r + 1, :]
            cy = gy + CURRENT_GAIN * currents[1, r : r + 1, :]
            flux = jnp.abs(cx) * (here - jnp.where(cx > 0.0, before, after))
            flux = flux + jnp.abs(cy) * (here - jnp.where(cy > 0.0, lines[r], lines[r + 2]))
            moved = mask[r : r + 1, :] * (here - flux)
            prop[r, part, :] = moved
            prop_16[part, r * cols : (r + 1) * cols] = moved.astype(jnp.bfloat16)
            growth = WIND_GAIN * jnp.maximum(
                wind[0, r : r + 1, :] * cos + wind[1, r : r + 1, :] * sin - phase, 0.0
            )
            pushed = growth * moved
            for value in (moved, ratio * moved, pushed * cos, pushed * sin):
                out.append(value.reshape(CHUNK // 8, 8, cols).sum(axis=0))
        return tuple(t + o for t, o in zip(totals, out))

    zero = jnp.zeros((8, cols), jnp.float32)
    totals = lax.fori_loop(0, comps // CHUNK, body, (zero,) * (4 * rows))
    for r in range(rows):
        for n in range(4):
            sums[n * rows + r : n * rows + r + 1, :] = totals[4 * r + n].sum(axis=0, keepdims=True)


def dot_0(left, right):
    return lax.dot_general(
        left, right, (((0,), (0,)), ((), ())), preferred_element_type=jnp.float32
    )


def own_kernel(first, prop_16, partial):
    comps = prop_16.shape[0]
    start = pl.multiple_of(lax.axis_index("comp") * comps, comps)
    partial[...] = dot_0(first[pl.ds(start, comps), :], prop_16[...])


def update_kernel(
    first, second, other_16, partial, prop, sums, other_sums, table, wind,
    state, low, high, ends, hidden, transfer,
):
    rows, comps, cols = prop.shape
    start = pl.multiple_of((1 - lax.axis_index("comp")) * comps, comps)
    scale_up = 2.0 * comps
    total = sums[...] + other_sums[...]
    floor = jnp.maximum(total[:rows, :], 1.0)
    spread_ratio = total[rows : 2 * rows, :] / floor
    squared = DECAY_GAIN * spread_ratio * spread_ratio
    gain = scale_up / floor
    back = NONLINEAR_GAIN * (floor / scale_up)
    pre = dot_0(first[pl.ds(start, comps), :], other_16[...]) + partial[...]
    pre = pre * jnp.concatenate([gain[r : r + 1, :] for r in range(rows)], axis=1)
    hidden[...] = (pre / (1.0 + jnp.exp(-pre))).astype(jnp.bfloat16)
    transfer[...] = dot_0(second[...], hidden[...]).astype(jnp.bfloat16)

    def body(i, carry):
        part = pl.ds(pl.multiple_of(i * CHUNK, CHUNK), CHUNK)
        tab = table[part, :]
        cos, sin, phase, ratio = (
            jnp.broadcast_to(tab[:, n : n + 1], (CHUNK, cols)) for n in range(2, 6)
        )
        for r in range(rows):
            growth = WIND_GAIN * jnp.maximum(
                wind[0, r : r + 1, :] * cos + wind[1, r : r + 1, :] * sin - phase, 0.0
            )
            fresh = prop[r, part, :] * jnp.exp(growth - ratio * squared[r : r + 1, :])
            fresh = fresh + back[r : r + 1, :] * transfer[part, r * cols : (r + 1) * cols].astype(
                jnp.float32
            )
            state[part, r, :] = fresh
            ends[part, r : r + 1] = fresh[:, :1]
            ends[part, rows + r : rows + r + 1] = fresh[:, cols - 1 :]
            if r == 0:
                low[part, :] = fresh.astype(jnp.bfloat16)
            if r == rows - 1:
                high[part, :] = fresh.astype(jnp.bfloat16)
        return carry

    lax.fori_loop(0, comps // CHUNK, body, 0)


def ocean_update(padded, stress, mask_f):

    def middle(field):
        return field[..., 1:-1, 1:-1]

    def eastern(field):
        return field[..., 1:-1, 2:]

    def western(field):
        return field[..., 1:-1, :-2]

    def northern(field):
        return field[..., 2:, 1:-1]

    def southern(field):
        return field[..., :-2, 1:-1]

    def spread(field):
        return (
            eastern(field)
            + western(field)
            + northern(field)
            + southern(field)
            - 4.0 * middle(field)
        )

    def column(field):
        upper_level = jnp.concatenate([field[:1], field[:-1]], axis=0)
        lower_level = jnp.concatenate([field[1:], field[-1:]], axis=0)
        return upper_level + lower_level - 2.0 * field

    density = -THERMAL * padded[2] + HALINE * padded[3]
    pressure = jnp.cumsum(density, axis=0) - 0.5 * density
    speed_u = middle(padded[0])
    speed_v = middle(padded[1])

    def carry_term(field):
        return speed_u * 0.5 * (eastern(field) - western(field)) + speed_v * 0.5 * (
            northern(field) - southern(field)
        )

    surface = (jnp.arange(padded.shape[1]) == 0).astype(jnp.float32)[:, None, None]
    tend_u = (
        CORIOLIS * speed_v
        - PRESSURE_GAIN * 0.5 * (eastern(pressure) - western(pressure))
        + LATERAL_MIX * spread(padded[0])
        + VERTICAL_MIX * column(speed_u)
        + STRESS_GAIN * surface * stress[0]
    )
    tend_v = (
        -CORIOLIS * speed_u
        - PRESSURE_GAIN * 0.5 * (northern(pressure) - southern(pressure))
        + LATERAL_MIX * spread(padded[1])
        + VERTICAL_MIX * column(speed_v)
        + STRESS_GAIN * surface * stress[1]
    )
    tend_t = (
        -ADVECTION * carry_term(padded[2])
        + LATERAL_MIX * spread(padded[2])
        + VERTICAL_MIX * column(middle(padded[2]))
    )
    tend_s = (
        -ADVECTION * carry_term(padded[3])
        + LATERAL_MIX * spread(padded[3])
        + VERTICAL_MIX * column(middle(padded[3]))
    )
    return middle(padded) + mask_f * jnp.stack([tend_u, tend_v, tend_t, tend_s])


def regrid(field, below, above, blocks, row_table):
    rows = field.shape[1]
    padded = jnp.concatenate([below, field, above], axis=1)
    first_row = lax.axis_index("gy") * rows
    offset = row_table[:, :, 0] - first_row - jnp.arange(rows)[:, None]
    offset = offset[None, :, :, None]
    selected = jnp.where(
        offset < 0,
        padded[:, :rows, None, :],
        jnp.where(offset == 0, padded[:, 1:-1, None, :], padded[:, 2:, None, :]),
    )
    return jnp.einsum("rbds,krbs->krd", blocks, selected, precision=lax.Precision.HIGHEST)


def local(
    spectra,
    wind_field,
    sea_mask,
    first_layer,
    second_layer,
    ocean_state,
    current_blocks,
    current_rows,
    stress_blocks,
    stress_rows,
):
    f32, b16 = jnp.float32, jnp.bfloat16
    mask_f = sea_mask.astype(f32)
    rows, cols = sea_mask.shape
    half_freqs, directions = spectra.shape[:2]
    comps = half_freqs * directions
    total = 2 * comps
    units = first_layer.shape[1]
    cells = rows * cols
    me = lax.axis_index("comp")
    table = lax.dynamic_slice_in_dim(
        jnp.asarray(tables(2 * half_freqs, directions)), me * comps, comps, 0
    )
    shape = jax.ShapeDtypeStruct
    edge_outs = (shape((comps, cols), b16), shape((comps, cols), b16), shape((comps, 2 * rows), f32))
    state = spectra.reshape(comps, rows, cols)
    low, high, ends = call(edges_kernel, edge_outs, moved=3 * comps * cells)(state)
    ocean_low, ocean_high = ocean_state[:, :, :1], ocean_state[:, :, -1:]
    ocean_south = from_lower(ocean_high, "gy")
    ocean_north = from_upper(ocean_low, "gy")
    ocean_west = from_lower(ocean_state[..., -1], "gx")[..., None]
    ocean_east = from_upper(ocean_state[..., 0], "gx")[..., None]
    currents = regrid(
        ocean_state[:2, 0], ocean_south[:2, 0], ocean_north[:2, 0], current_blocks, current_rows
    )
    second_own = lax.dynamic_slice_in_dim(second_layer, me * comps, comps, 1)
    pushes = jnp.zeros((2 * rows, cols), f32)
    for step in range(STEPS):
        south = from_lower(high, "gy")
        north = from_upper(low, "gy")
        flipped = ends.T
        west = from_lower(flipped[rows:], "gx").T
        east = from_upper(flipped[:rows], "gx").T
        prop, prop_16, sums = call(
            advect_kernel,
            (shape((rows, comps, cols), f32), shape((comps, cells), b16), shape((4 * rows, cols), f32)),
            flops=40 * comps * cells,
            moved=12 * comps * cells,
        )(state, south, north, west, east, table, currents, wind_field, mask_f)
        other_sums = partner_of(sums)
        other_16 = partner_of(prop_16)
        partial = call(
            own_kernel,
            shape((units, cells), f32),
            flops=2 * comps * units * cells,
            moved=4 * units * cells + 4 * comps * units,
        )(first_layer, prop_16)
        state, low, high, ends = call(
            update_kernel,
            (shape((comps, rows, cols), f32),) + edge_outs,
            scratch=(pltpu.VMEM((units, cells), b16), pltpu.VMEM((comps, cells), b16)),
            flops=4 * comps * units * cells,
            moved=16 * comps * cells,
        )(first_layer, second_own, other_16, partial, prop, sums, other_sums, table, wind_field)
        pushes = pushes + sums[2 * rows :] + other_sums[2 * rows :]
    stress = (pushes / (STEPS * total)).reshape(2, rows, cols)
    stress_ocean = regrid(
        stress,
        from_lower(stress[:, -1:], "gy"),
        from_upper(stress[:, :1], "gy"),
        stress_blocks,
        stress_rows,
    )
    corner = jnp.zeros(ocean_west.shape[:2] + (1, 1), f32)
    padded = jnp.concatenate(
        [
            jnp.concatenate([corner, ocean_south, corner], axis=3),
            jnp.concatenate([ocean_west, ocean_state, ocean_east], axis=3),
            jnp.concatenate([corner, ocean_north, corner], axis=3),
        ],
        axis=2,
    )
    return (state.reshape(spectra.shape), ocean_update(padded, stress_ocean, mask_f))


def solution(mesh):
    placed = (
        P("comp", None, "gy", "gx"),
        P(None, "gy", "gx"),
        P("gy", "gx"),
        P(),
        P(),
        P(None, None, "gy", "gx"),
        P("gy", None, "gx", None),
        P("gy", None, "gx"),
        P("gy", None, "gx", None),
        P("gy", None, "gx"),
    )
    return jax.shard_map(
        local,
        mesh=mesh,
        in_specs=placed,
        out_specs=(P("comp", None, "gy", "gx"), P(None, None, "gy", "gx")),
        check_vma=False,
    )
```

time: 249 us -> 120 us (0.48)
  the two profiles are of different devices: /device:TPU:0 before, /device:TPU:29 now
where the time goes in v1:
time: 120 us; the launch traced here: 119 us
  Pallas kernels  42.3 us (35%)
  starting transfers between devices  41.5 us (35%)
  waiting for transfers between devices  16.7 us (14%)
  local copies, waits for them, and re-layouts  12.3 us (10%)
  other arithmetic  3.58 us (3%)
  matrix products  1.74 us (1%)
    ppermute x7, starting transfers between devices, from_upper(): return lax.ppermute(block, axis, [(i + 1, i) for i in range(count - 1)])  24.7 us
    pallas_call x2, Pallas kernels, local(): call(update_kernel, (shape((comps, rows, cols), f32),) + edge_outs, scrat...  18.4 us
    ppermute x7, starting transfers between devices, from_lower(): return lax.ppermute(block, axis, [(i, i + 1) for i in range(count - 1)])  13.8 us
    pallas_call x2, Pallas kernels, local(): call(advect_kernel, (shape((rows, comps, cols), f32), shape((comps, cells...  11.6 us
    pallas_call x2, Pallas kernels, local(): call(own_kernel, shape((units, cells), f32), flops=2 * comps * units * ce...  8.29 us
    ppermute x4, waiting for transfers between devices, partner_of(): return lax.ppermute(block, 'comp', [(0, 1), (1, 0)])  7.75 us
    ppermute x7, waiting for transfers between devices, from_upper(): return lax.ppermute(block, axis, [(i + 1, i) for i in range(count - 1)])  7.46 us
    pallas_call x1, Pallas kernels, local(): call(edges_kernel, edge_outs, moved=3 * comps * cells)(state)  4.03 us
  transfers between devices with their start and end apart: 18, of which 5 were waited for; matrix products, arithmetic and copies ran while one was open for 12% of the time, Pallas kernels for 7%

profile of v1, /device:TPU:29, one launch (start us, length us, event | category | flops | bytes accessed | tf_op | source)
XLA Modules:
  0.0 119.3 jit_solution(7594464161004867626)
XLA Ops:
  0.7 4.0 %shard_map.122 = (bf16[576,128]{1,0:T(8,128)(2,1)}, bf16[576,128]{1,0:T(8,128)(2,1)}, f32[576,8]{1,0:T(8,128)}) custom-call(f32[576,4,128]{2,1,0:T(4,128)} %bitcast.68), custom_call_target="tpu_custom_call" | custom-call | bytes 884736 | tf_op jit(solution)/shard_map/pallas_call | solution.py:289
  4.7 1.4 %collective-permute-start = (bf16[576,128]{1,0:T(8,128)(2,1)}, bf16[576,128]{1,0:T(8,128)(2,1)S(1)}, u32[]{:S(2)}, u32[]{:S(2)}) collective-permute-start(bf16[576,128]{1,0:T(8,128)(2,1)} %get-tuple-element.16), channel_id=1, source_target_pairs={{0,4},{4,8},{8,12},{1,5},{5,9},{9,13},{2,6},{6,10},{10,14},{3,7},{... | collective-permute-start | bytes 442376 | tf_op jit(solution)/shard_map/ppermute | solution.py:29
  6.1 1.7 %fusion.67 = (f32[4,16,1,128]{3,2,1,0:T(1,128)}, f32[4,16,1,128]{3,2,1,0:T(1,128)S(1)}) fusion(f32[4,16,4,128]{3,2,1,0:T(4,128)} %param.16), kind=kLoop, calls=%fused_computation.105 | loop fusion | bytes 131072 | tf_op jit(solution)/shard_map/slice | solution.py:290
  7.8 1.3 %collective-permute-start.4 = (f32[4,16,1,128]{3,2,1,0:T(1,128)}, f32[4,16,1,128]{3,2,1,0:T(1,128)S(1)}, u32[]{:S(2)}, u32[]{:S(2)}) collective-permute-start(f32[4,16,1,128]{3,2,1,0:T(1,128)} %get-tuple-element.56), channel_id=1, source_target_pairs={{0,4},{4,8},{8,12},{1,5},{5,9},{9,13},{2,6},{6,10},{10,14},{3,7},{... | collective-permute-start | bytes 98312 | tf_op jit(solution)/shard_map/ppermute | solution.py:29
  9.0 4.6 %collective-permute-start.5 = (f32[4,16,1,128]{3,2,1,0:T(1,128)S(1)}, f32[4,16,1,128]{3,2,1,0:T(1,128)S(1)}, u32[]{:S(2)}, u32[]{:S(2)}) collective-permute-start(f32[4,16,1,128]{3,2,1,0:T(1,128)S(1)} %get-tuple-element.57), channel_id=1, source_target_pairs={{4,0},{8,4},{12,8},{5,1},{9,5},{13,9},{6,2},{10,6},{14,10},{7,3},{... | collective-permute-start | bytes 98312 | tf_op jit(solution)/shard_map/ppermute | solution.py:34
  14.0 3.2 %collective-permute-start.15 = (f32[4,16,4]{1,2,0:T(4,128)S(1)}, f32[4,16,4]{1,2,0:T(4,128)S(1)}, u32[]{:S(2)}, u32[]{:S(2)}) collective-permute-start(f32[4,16,4]{1,2,0:T(4,128)S(1)} %bitcast.85), channel_id=1, source_target_pairs={{1,0},{2,1},{3,2},{5,4},{6,5},{7,6},{9,8},{10,9},{11,10},{13,12},{... | collective-permute-start | bytes 3080 | tf_op jit(solution)/shard_map/ppermute | solution.py:34
  17.3 3.0 %collective-permute-start.14 = (f32[4,16,4]{1,2,0:T(4,128)S(1)}, f32[4,16,4]{1,2,0:T(4,128)S(1)}, u32[]{:S(2)}, u32[]{:S(2)}) collective-permute-start(f32[4,16,4]{1,2,0:T(4,128)S(1)} %bitcast.84), channel_id=1, source_target_pairs={{0,1},{1,2},{2,3},{4,5},{5,6},{6,7},{8,9},{9,10},{10,11},{12,13},{... | collective-permute-start | bytes 3080 | tf_op jit(solution)/shard_map/ppermute | solution.py:29
  21.3 1.7 %constant_dynamic-slice_fusion.1.second = bf16[1024,576]{1,0:T(8,128)(2,1)} fusion(bf16[1024,1152]{1,0:T(8,128)(2,1)S(1)} %copy-done, s32[]{:T(128)S(6)} %select_n.18), kind=kLoop, calls=%fused_computation.91 | loop fusion | bytes 2359300 | tf_op jit(solution)/shard_map/dynamic_slice | solution.py:298
  25.3 4.3 %collective-permute-start.1 = (bf16[576,128]{1,0:T(8,128)(2,1)}, bf16[576,128]{1,0:T(8,128)(2,1)}, u32[]{:S(2)}, u32[]{:S(2)}) collective-permute-start(bf16[576,128]{1,0:T(8,128)(2,1)} %get-tuple-element.17), channel_id=1, source_target_pairs={{4,0},{8,4},{12,8},{5,1},{9,5},{13,9},{6,2},{10,6},{14,10},{7,3},{... | collective-permute-start | bytes 442376 | tf_op jit(solution)/shard_map/ppermute | solution.py:34
  29.8 2.7 %collective-permute-start.2 = (f32[4,576]{0,1:T(8,128)}, f32[4,576]{0,1:T(8,128)}, u32[]{:S(2)}, u32[]{:S(2)}) collective-permute-start(f32[4,576]{0,1:T(8,128)} %get-tuple-element.37), channel_id=1, source_target_pairs={{0,1},{1,2},{2,3},{4,5},{5,6},{6,7},{8,9},{9,10},{10,11},{12,13},{... | collective-permute-start | bytes 27656 | tf_op jit(solution)/shard_map/ppermute | solution.py:29
  32.7 2.4 %collective-permute-start.3 = (f32[4,576]{0,1:T(8,128)}, f32[4,576]{0,1:T(8,128)S(1)}, u32[]{:S(2)}, u32[]{:S(2)}) collective-permute-start(f32[4,576]{0,1:T(8,128)} %get-tuple-element.36), channel_id=1, source_target_pairs={{1,0},{2,1},{3,2},{5,4},{6,5},{7,6},{9,8},{10,9},{11,10},{13,12},{... | collective-permute-start | bytes 27656 | tf_op jit(solution)/shard_map/ppermute | solution.py:34
  36.1 1.2 convolution_bitcast_fusion.1
  37.9 3.0 %collective-permute-done.3 = f32[4,576]{0,1:T(8,128)S(1)} collective-permute-done((f32[4,576]{0,1:T(8,128)}, f32[4,576]{0,1:T(8,128)S(1)}, u32[]{:S(2)}, u32[]{:S(2)}) %collective-permute-start.3) | collective-permute-done | bytes 9248 | tf_op jit(solution)/shard_map/ppermute | solution.py:34
  41.7 5.8 %shard_map.123 = (f32[4,576,128]{2,1,0:T(8,128)}, bf16[576,512]{1,0:T(8,128)(2,1)}, f32[16,128]{1,0:T(8,128)}) custom-call(f32[576,4,128]{2,1,0:T(4,128)} %bitcast.69, bf16[576,128]{1,0:T(8,128)(2,1)} %copy-done.11, bf16[576,128]{1,0:T(8,128)(2,1)} %collective-permute-done.1.north, f32[576,4]{1,0:T(8,128)} %bitcast.2.west, f32[576,4]{1,0:T(8,128)} %bitcast.72, ...), custom_call_target="tpu_custom_call" | custom-call | flops 11796480 | bytes 3538944 | tf_op jit(solution)/shard_map/pallas_call | solution.py:306
  48.2 1.3 %collective-permute-start.7 = (f32[16,128]{1,0:T(8,128)}, f32[16,128]{1,0:T(8,128)S(1)}, u32[]{:S(2)}, u32[]{:S(2)}) collective-permute-start(f32[16,128]{1,0:T(8,128)} %get-tuple-element.21.sums), channel_id=1, source_target_pairs={{0,16},{16,0},{1,17},{17,1},{2,18},{18,2},{3,19},{19,3},{4,20},{20... | collective-permute-start | bytes 24584 | tf_op jit(solution)/shard_map/ppermute | solution.py:38
  49.5 4.1 %shard_map.124.partial = f32[1024,512]{1,0:T(8,128)} custom-call(bf16[1152,1024]{1,0:T(8,128)(2,1)} %first.7, bf16[576,512]{1,0:T(8,128)(2,1)} %get-tuple-element.19.prop_16), custom_call_target="tpu_custom_call" | custom-call | flops 603979776 | bytes 4456448 | tf_op jit(solution)/shard_map/pallas_call | solution.py:314
  53.6 6.1 %collective-permute-done.7.other_sums = f32[16,128]{1,0:T(8,128)S(1)} collective-permute-done((f32[16,128]{1,0:T(8,128)}, f32[16,128]{1,0:T(8,128)S(1)}, u32[]{:S(2)}, u32[]{:S(2)}) %collective-permute-start.7) | collective-permute-done | bytes 8224 | tf_op jit(solution)/shard_map/ppermute | solution.py:38
  60.6 9.2 %shard_map.125 = (f32[576,4,128]{2,1,0:T(4,128)}, bf16[576,128]{1,0:T(8,128)(2,1)}, bf16[576,128]{1,0:T(8,128)(2,1)}, f32[576,8]{1,0:T(8,128)}) custom-call(bf16[1152,1024]{1,0:T(8,128)(2,1)} %first.7, bf16[1024,576]{1,0:T(8,128)(2,1)} %constant_dynamic-slice_fusion.1.second, bf16[576,512]{1,0:T(8,128)(2,1)} %copy-done.4, f32[1024,512]{1,0:T(8,128)} %shard_map.124.partial, ...), custom_call_target="tpu_custom_call" | custom-call | flops 1207959552 | bytes 4718592 | tf_op jit(solution)/shard_map/pallas_call | solution.py:320
  69.8 1.3 %collective-permute-start.8 = (bf16[576,128]{1,0:T(8,128)(2,1)}, bf16[576,128]{1,0:T(8,128)(2,1)S(1)}, u32[]{:S(2)}, u32[]{:S(2)}) collective-permute-start(bf16[576,128]{1,0:T(8,128)(2,1)} %get-tuple-element.23), channel_id=1, source_target_pairs={{0,4},{4,8},{8,12},{1,5},{5,9},{9,13},{2,6},{6,10},{10,14},{3,7},{... | collective-permute-start | bytes 442376 | tf_op jit(solution)/shard_map/ppermute | solution.py:29
  71.1 4.0 %collective-permute-start.9 = (bf16[576,128]{1,0:T(8,128)(2,1)}, bf16[576,128]{1,0:T(8,128)(2,1)S(1)}, u32[]{:S(2)}, u32[]{:S(2)}) collective-permute-start(bf16[576,128]{1,0:T(8,128)(2,1)} %get-tuple-element.24), channel_id=1, source_target_pairs={{4,0},{8,4},{12,8},{5,1},{9,5},{13,9},{6,2},{10,6},{14,10},{7,3},{... | collective-permute-start | bytes 442376 | tf_op jit(solution)/shard_map/ppermute | solution.py:34
  75.1 1.2 fusion.56
  76.3 2.9 %collective-permute-start.10 = (f32[4,576]{0,1:T(8,128)S(1)}, f32[4,576]{0,1:T(8,128)S(1)}, u32[]{:S(2)}, u32[]{:S(2)}) collective-permute-start(f32[4,576]{0,1:T(8,128)S(1)} %get-tuple-element.35), channel_id=1, source_target_pairs={{0,1},{1,2},{2,3},{4,5},{5,6},{6,7},{8,9},{9,10},{10,11},{12,13},{... | collective-permute-start | bytes 27656 | tf_op jit(solution)/shard_map/ppermute | solution.py:29
  79.2 1.9 %collective-permute-start.11 = (f32[4,576]{0,1:T(8,128)S(1)}, f32[4,576]{0,1:T(8,128)S(1)}, u32[]{:S(2)}, u32[]{:S(2)}) collective-permute-start(f32[4,576]{0,1:T(8,128)S(1)} %get-tuple-element.34), channel_id=1, source_target_pairs={{1,0},{2,1},{3,2},{5,4},{6,5},{7,6},{9,8},{10,9},{11,10},{13,12},{... | collective-permute-start | bytes 27656 | tf_op jit(solution)/shard_map/ppermute | solution.py:34
  81.3 1.5 %collective-permute-done.10 = f32[4,576]{0,1:T(8,128)S(1)} collective-permute-done((f32[4,576]{0,1:T(8,128)S(1)}, f32[4,576]{0,1:T(8,128)S(1)}, u32[]{:S(2)}, u32[]{:S(2)}) %collective-permute-start.10) | collective-permute-done | bytes 9248 | tf_op jit(solution)/shard_map/ppermute | solution.py:29
  82.8 4.4 %collective-permute-done.11 = f32[4,576]{0,1:T(8,128)S(1)} collective-permute-done((f32[4,576]{0,1:T(8,128)S(1)}, f32[4,576]{0,1:T(8,128)S(1)}, u32[]{:S(2)}, u32[]{:S(2)}) %collective-permute-start.11) | collective-permute-done | bytes 9248 | tf_op jit(solution)/shard_map/ppermute | solution.py:34
  88.1 5.8 %shard_map.126 = (f32[4,576,128]{2,1,0:T(8,128)}, bf16[576,512]{1,0:T(8,128)(2,1)}, f32[16,128]{1,0:T(8,128)}) custom-call(f32[576,4,128]{2,1,0:T(4,128)} %get-tuple-element.22.state, bf16[576,128]{1,0:T(8,128)(2,1)} %copy-done.12, bf16[576,128]{1,0:T(8,128)(2,1)} %copy-done.13, f32[576,4]{1,0:T(8,128)} %bitcast.73, f32[576,4]{1,0:T(8,128)} %bitcast.74, ...), custom_call_target="tpu_custom_call" | custom-call | flops 11796480 | bytes 3538944 | tf_op jit(solution)/shard_map/pallas_call | solution.py:306
  94.2 1.3 %collective-permute-start.12 = (bf16[576,512]{1,0:T(8,128)(2,1)}, bf16[576,512]{1,0:T(8,128)(2,1)S(1)}, u32[]{:S(2)}, u32[]{:S(2)}) collective-permute-start(bf16[576,512]{1,0:T(8,128)(2,1)} %get-tuple-element.26.prop_16), channel_id=1, source_target_pairs={{0,16},{16,0},{1,17},{17,1},{2,18},{18,2},{3,19},{19,3},{4,20},{20... | collective-permute-start | bytes 1769480 | tf_op jit(solution)/shard_map/ppermute | solution.py:38
  95.4 1.6 %collective-permute-done.13.other_sums = f32[16,128]{1,0:T(8,128)S(1)} collective-permute-done((f32[16,128]{1,0:T(8,128)}, f32[16,128]{1,0:T(8,128)S(1)}, u32[]{:S(2)}, u32[]{:S(2)}) %collective-permute-start.13) | collective-permute-done | bytes 8224 | tf_op jit(solution)/shard_map/ppermute | solution.py:38
  97.8 1.3 %collective-permute-start.16 = (f32[2,1,128]{2,1,0:T(1,128)S(1)}, f32[2,1,128]{2,1,0:T(1,128)S(1)}, u32[]{:S(2)}, u32[]{:S(2)}) collective-permute-start(f32[2,1,128]{2,1,0:T(1,128)S(1)} %get-tuple-element.62), channel_id=1, source_target_pairs={{0,4},{4,8},{8,12},{1,5},{5,9},{9,13},{2,6},{6,10},{10,14},{3,7},{... | collective-permute-start | bytes 3080 | tf_op jit(solution)/shard_map/ppermute | solution.py:29
  99.1 4.3 %collective-permute-start.17 = (f32[2,1,128]{2,1,0:T(1,128)S(1)}, f32[2,1,128]{2,1,0:T(1,128)S(1)}, u32[]{:S(2)}, u32[]{:S(2)}) collective-permute-start(f32[2,1,128]{2,1,0:T(1,128)S(1)} %get-tuple-element.63), channel_id=1, source_target_pairs={{4,0},{8,4},{12,8},{5,1},{9,5},{13,9},{6,2},{10,6},{14,10},{7,3},{... | collective-permute-start | bytes 3080 | tf_op jit(solution)/shard_map/ppermute | solution.py:34
  103.4 4.1 %shard_map.127.partial = f32[1024,512]{1,0:T(8,128)} custom-call(bf16[1152,1024]{1,0:T(8,128)(2,1)} %first.7, bf16[576,512]{1,0:T(8,128)(2,1)} %get-tuple-element.26.prop_16), custom_call_target="tpu_custom_call" | custom-call | flops 603979776 | bytes 4456448 | tf_op jit(solution)/shard_map/pallas_call | solution.py:314
  110.2 9.2 %shard_map.128 = (f32[576,4,128]{2,1,0:T(4,128)}, bf16[576,128]{1,0:T(8,128)(2,1)}, bf16[576,128]{1,0:T(8,128)(2,1)}, f32[576,8]{1,0:T(8,128)}) custom-call(bf16[1152,1024]{1,0:T(8,128)(2,1)} %first.7, bf16[1024,576]{1,0:T(8,128)(2,1)} %constant_dynamic-slice_fusion.1.second, bf16[576,512]{1,0:T(8,128)(2,1)} %copy-done.3, f32[1024,512]{1,0:T(8,128)} %shard_map.127.partial, ...), custom_call_target="tpu_custom_call" | custom-call | flops 1207959552 | bytes 4718592 | tf_op jit(solution)/shard_map/pallas_call | solution.py:320
  (104 shorter events, 12.4 us)
Async XLA Ops:
  0.6 20.6 %copy-start = (bf16[1024,1152]{1,0:T(8,128)(2,1)S(1)}, bf16[1024,1152]{1,0:T(8,128)(2,1)}, u32[]{:S(2)}) copy-start(bf16[1024,1152]{1,0:T(8,128)(2,1)} %param.15) | copy-start | bytes 7077892
  0.6 13.0 %copy-start.1 = (f32[4,16,4,128]{3,2,1,0:T(4,128)S(1)}, f32[4,16,4,128]{3,2,1,0:T(4,128)}, u32[]{:S(2)}) copy-start(f32[4,16,4,128]{3,2,1,0:T(4,128)} %param.16) | copy-start | bytes 393220
  4.7 15.7 %copy-start.2 = (f32[576,8]{1,0:T(8,128)S(1)}, f32[576,8]{1,0:T(8,128)}, u32[]{:S(2)}) copy-start(f32[576,8]{1,0:T(8,128)} %get-tuple-element.18) | copy-start | bytes 55300
  4.7 36.3 %collective-permute-start = (bf16[576,128]{1,0:T(8,128)(2,1)}, bf16[576,128]{1,0:T(8,128)(2,1)S(1)}, u32[]{:S(2)}, u32[]{:S(2)}) collective-permute-start(bf16[576,128]{1,0:T(8,128)(2,1)} %get-tuple-element.16), channel_id=1, source_target_pairs={{0,4},{4,8},{8,12},{1,5},{5,9},{9,13},{2,6},{6,10},{10,14},{3,7},{... | collective-permute-start | bytes 442376 | tf_op jit(solution)/shard_map/ppermute | solution.py:29
  7.8 24.9 %collective-permute-start.4 = (f32[4,16,1,128]{3,2,1,0:T(1,128)}, f32[4,16,1,128]{3,2,1,0:T(1,128)S(1)}, u32[]{:S(2)}, u32[]{:S(2)}) collective-permute-start(f32[4,16,1,128]{3,2,1,0:T(1,128)} %get-tuple-element.56), channel_id=1, source_target_pairs={{0,4},{4,8},{8,12},{1,5},{5,9},{9,13},{2,6},{6,10},{10,14},{3,7},{... | collective-permute-start | bytes 98312 | tf_op jit(solution)/shard_map/ppermute | solution.py:29
  9.0 26.0 %collective-permute-start.5 = (f32[4,16,1,128]{3,2,1,0:T(1,128)S(1)}, f32[4,16,1,128]{3,2,1,0:T(1,128)S(1)}, u32[]{:S(2)}, u32[]{:S(2)}) collective-permute-start(f32[4,16,1,128]{3,2,1,0:T(1,128)S(1)} %get-tuple-element.57), channel_id=1, source_target_pairs={{4,0},{8,4},{12,8},{5,1},{9,5},{13,9},{6,2},{10,6},{14,10},{7,3},{... | collective-permute-start | bytes 98312 | tf_op jit(solution)/shard_map/ppermute | solution.py:34
  14.0 11.3 %collective-permute-start.15 = (f32[4,16,4]{1,2,0:T(4,128)S(1)}, f32[4,16,4]{1,2,0:T(4,128)S(1)}, u32[]{:S(2)}, u32[]{:S(2)}) collective-permute-start(f32[4,16,4]{1,2,0:T(4,128)S(1)} %bitcast.85), channel_id=1, source_target_pairs={{1,0},{2,1},{3,2},{5,4},{6,5},{7,6},{9,8},{10,9},{11,10},{13,12},{... | collective-permute-start | bytes 3080 | tf_op jit(solution)/shard_map/ppermute | solution.py:34
  17.3 12.5 %collective-permute-start.14 = (f32[4,16,4]{1,2,0:T(4,128)S(1)}, f32[4,16,4]{1,2,0:T(4,128)S(1)}, u32[]{:S(2)}, u32[]{:S(2)}) collective-permute-start(f32[4,16,4]{1,2,0:T(4,128)S(1)} %bitcast.84), channel_id=1, source_target_pairs={{0,1},{1,2},{2,3},{4,5},{5,6},{6,7},{8,9},{9,10},{10,11},{12,13},{... | collective-permute-start | bytes 3080 | tf_op jit(solution)/shard_map/ppermute | solution.py:29
  21.3 1.7 %copy-start.10 = (f32[1152,8]{1,0:T(8,128)S(1)}, f32[1152,8]{1,0:T(8,128)}, u32[]{:S(2)}) copy-start(f32[1152,8]{1,0:T(8,128)} %constant.53.clone) | copy-start | bytes 110596
  21.3 2.5 %copy-start.20 = (s32[4,2,1]{0,2,1:T(1,128)S(1)}, s32[4,2,1]{0,2,1:T(1,128)}, u32[]{:S(2)}) copy-start(s32[4,2,1]{0,2,1:T(1,128)} %param.20) | copy-start | bytes 100
  21.3 2.5 %copy-start.21 = (s32[4,2,1]{0,2,1:T(1,128)S(1)}, s32[4,2,1]{0,2,1:T(1,128)}, u32[]{:S(2)}) copy-start(s32[4,2,1]{0,2,1:T(1,128)} %param.18) | copy-start | bytes 100
  21.3 3.2 %copy-start.19 = (s32[4,128]{1,0:T(4,128)S(1)}, s32[4,128]{1,0:T(4,128)}, u32[]{:S(2)}) copy-start(s32[4,128]{1,0:T(4,128)} %param.13) | copy-start | bytes 6148
  25.3 15.6 %collective-permute-start.1 = (bf16[576,128]{1,0:T(8,128)(2,1)}, bf16[576,128]{1,0:T(8,128)(2,1)}, u32[]{:S(2)}, u32[]{:S(2)}) collective-permute-start(bf16[576,128]{1,0:T(8,128)(2,1)} %get-tuple-element.17), channel_id=1, source_target_pairs={{4,0},{8,4},{12,8},{5,1},{9,5},{13,9},{6,2},{10,6},{14,10},{7,3},{... | collective-permute-start | bytes 442376 | tf_op jit(solution)/shard_map/ppermute | solution.py:34
  29.6 6.4 %copy-start.5 = (f32[4,2,128,128]{3,2,1,0:T(8,128)S(1)}, f32[4,2,128,128]{3,2,1,0:T(8,128)}, u32[]{:S(2)}) copy-start(f32[4,2,128,128]{3,2,1,0:T(8,128)} %param.17) | copy-start | bytes 1572868
  29.8 8.1 %collective-permute-start.2 = (f32[4,576]{0,1:T(8,128)}, f32[4,576]{0,1:T(8,128)}, u32[]{:S(2)}, u32[]{:S(2)}) collective-permute-start(f32[4,576]{0,1:T(8,128)} %get-tuple-element.37), channel_id=1, source_target_pairs={{0,1},{1,2},{2,3},{4,5},{5,6},{6,7},{8,9},{9,10},{10,11},{12,13},{... | collective-permute-start | bytes 27656 | tf_op jit(solution)/shard_map/ppermute | solution.py:29
  32.7 8.3 %collective-permute-start.3 = (f32[4,576]{0,1:T(8,128)}, f32[4,576]{0,1:T(8,128)S(1)}, u32[]{:S(2)}, u32[]{:S(2)}) collective-permute-start(f32[4,576]{0,1:T(8,128)} %get-tuple-element.36), channel_id=1, source_target_pairs={{1,0},{2,1},{3,2},{5,4},{6,5},{7,6},{9,8},{10,9},{11,10},{13,12},{... | collective-permute-start | bytes 27656 | tf_op jit(solution)/shard_map/ppermute | solution.py:34
  47.5 12.2 %collective-permute-start.6 = (bf16[576,512]{1,0:T(8,128)(2,1)}, bf16[576,512]{1,0:T(8,128)(2,1)S(1)}, u32[]{:S(2)}, u32[]{:S(2)}) collective-permute-start(bf16[576,512]{1,0:T(8,128)(2,1)} %get-tuple-element.19.prop_16), channel_id=1, source_target_pairs={{0,16},{16,0},{1,17},{17,1},{2,18},{18,2},{3,19},{19,3},{4,20},{20... | collective-permute-start | bytes 1769480 | tf_op jit(solution)/shard_map/ppermute | solution.py:38
  48.2 11.6 %collective-permute-start.7 = (f32[16,128]{1,0:T(8,128)}, f32[16,128]{1,0:T(8,128)S(1)}, u32[]{:S(2)}, u32[]{:S(2)}) collective-permute-start(f32[16,128]{1,0:T(8,128)} %get-tuple-element.21.sums), channel_id=1, source_target_pairs={{0,16},{16,0},{1,17},{17,1},{2,18},{18,2},{3,19},{19,3},{4,20},{20... | collective-permute-start | bytes 24584 | tf_op jit(solution)/shard_map/ppermute | solution.py:38
  69.8 17.4 %collective-permute-start.8 = (bf16[576,128]{1,0:T(8,128)(2,1)}, bf16[576,128]{1,0:T(8,128)(2,1)S(1)}, u32[]{:S(2)}, u32[]{:S(2)}) collective-permute-start(bf16[576,128]{1,0:T(8,128)(2,1)} %get-tuple-element.23), channel_id=1, source_target_pairs={{0,4},{4,8},{8,12},{1,5},{5,9},{9,13},{2,6},{6,10},{10,14},{3,7},{... | collective-permute-start | bytes 442376 | tf_op jit(solution)/shard_map/ppermute | solution.py:29
  71.1 16.1 %collective-permute-start.9 = (bf16[576,128]{1,0:T(8,128)(2,1)}, bf16[576,128]{1,0:T(8,128)(2,1)S(1)}, u32[]{:S(2)}, u32[]{:S(2)}) collective-permute-start(bf16[576,128]{1,0:T(8,128)(2,1)} %get-tuple-element.24), channel_id=1, source_target_pairs={{4,0},{8,4},{12,8},{5,1},{9,5},{13,9},{6,2},{10,6},{14,10},{7,3},{... | collective-permute-start | bytes 442376 | tf_op jit(solution)/shard_map/ppermute | solution.py:34
  76.3 6.5 %collective-permute-start.10 = (f32[4,576]{0,1:T(8,128)S(1)}, f32[4,576]{0,1:T(8,128)S(1)}, u32[]{:S(2)}, u32[]{:S(2)}) collective-permute-start(f32[4,576]{0,1:T(8,128)S(1)} %get-tuple-element.35), channel_id=1, source_target_pairs={{0,1},{1,2},{2,3},{4,5},{5,6},{6,7},{8,9},{9,10},{10,11},{12,13},{... | collective-permute-start | bytes 27656 | tf_op jit(solution)/shard_map/ppermute | solution.py:29
  79.2 8.0 %collective-permute-start.11 = (f32[4,576]{0,1:T(8,128)S(1)}, f32[4,576]{0,1:T(8,128)S(1)}, u32[]{:S(2)}, u32[]{:S(2)}) collective-permute-start(f32[4,576]{0,1:T(8,128)S(1)} %get-tuple-element.34), channel_id=1, source_target_pairs={{1,0},{2,1},{3,2},{5,4},{6,5},{7,6},{9,8},{10,9},{11,10},{13,12},{... | collective-permute-start | bytes 27656 | tf_op jit(solution)/shard_map/ppermute | solution.py:34
  81.1 15.9 %copy-start.15 = (f32[16,128]{1,0:T(8,128)S(1)}, f32[16,128]{1,0:T(8,128)}, u32[]{:S(2)}) copy-start(f32[16,128]{1,0:T(8,128)} %get-tuple-element.21.sums) | copy-start | bytes 24580
  81.1 15.9 %copy-start.18 = (f32[16,128]{1,0:T(8,128)S(1)}, f32[16,128]{1,0:T(8,128)}, u32[]{:S(2)}) copy-start(f32[16,128]{1,0:T(8,128)} %copy-done.17) | copy-start | bytes 24580
  82.8 4.4 %copy-start.8 = (f32[4,576]{0,1:T(8,128)}, f32[4,576]{0,1:T(8,128)S(1)}, u32[]{:S(2)}) copy-start(f32[4,576]{0,1:T(8,128)S(1)} %collective-permute-done.10) | copy-start | bytes 27652
  93.9 3.2 %collective-permute-start.13 = (f32[16,128]{1,0:T(8,128)}, f32[16,128]{1,0:T(8,128)S(1)}, u32[]{:S(2)}, u32[]{:S(2)}) collective-permute-start(f32[16,128]{1,0:T(8,128)} %get-tuple-element.28.sums), channel_id=1, source_target_pairs={{0,16},{16,0},{1,17},{17,1},{2,18},{18,2},{3,19},{19,3},{4,20},{20... | collective-permute-start | bytes 24584 | tf_op jit(solution)/shard_map/ppermute | solution.py:38
  94.2 15.1 %collective-permute-start.12 = (bf16[576,512]{1,0:T(8,128)(2,1)}, bf16[576,512]{1,0:T(8,128)(2,1)S(1)}, u32[]{:S(2)}, u32[]{:S(2)}) collective-permute-start(bf16[576,512]{1,0:T(8,128)(2,1)} %get-tuple-element.26.prop_16), channel_id=1, source_target_pairs={{0,16},{16,0},{1,17},{17,1},{2,18},{18,2},{3,19},{19,3},{4,20},{20... | collective-permute-start | bytes 1769480 | tf_op jit(solution)/shard_map/ppermute | solution.py:38
  97.1 10.5 %copy-start.16 = (f32[16,128]{1,0:T(8,128)}, f32[16,128]{1,0:T(8,128)S(1)}, u32[]{:S(2)}) copy-start(f32[16,128]{1,0:T(8,128)S(1)} %collective-permute-done.13.other_sums) | copy-start | bytes 24580
  97.8 9.8 %collective-permute-start.16 = (f32[2,1,128]{2,1,0:T(1,128)S(1)}, f32[2,1,128]{2,1,0:T(1,128)S(1)}, u32[]{:S(2)}, u32[]{:S(2)}) collective-permute-start(f32[2,1,128]{2,1,0:T(1,128)S(1)} %get-tuple-element.62), channel_id=1, source_target_pairs={{0,4},{4,8},{8,12},{1,5},{5,9},{9,13},{2,6},{6,10},{10,14},{3,7},{... | collective-permute-start | bytes 3080 | tf_op jit(solution)/shard_map/ppermute | solution.py:29
  99.0 8.5 %copy-start.6 = (f32[4,2,128,128]{3,2,1,0:T(8,128)S(1)}, f32[4,2,128,128]{3,2,1,0:T(8,128)}, u32[]{:S(2)}) copy-start(f32[4,2,128,128]{3,2,1,0:T(8,128)} %param.19) | copy-start | bytes 1572868
  99.1 8.5 %collective-permute-start.17 = (f32[2,1,128]{2,1,0:T(1,128)S(1)}, f32[2,1,128]{2,1,0:T(1,128)S(1)}, u32[]{:S(2)}, u32[]{:S(2)}) collective-permute-start(f32[2,1,128]{2,1,0:T(1,128)S(1)} %get-tuple-element.63), channel_id=1, source_target_pairs={{4,0},{8,4},{12,8},{5,1},{9,5},{13,9},{6,2},{10,6},{14,10},{7,3},{... | collective-permute-start | bytes 3080 | tf_op jit(solution)/shard_map/ppermute | solution.py:34
  107.5 1.1 copy-start.14
  (8 other events, 6.1 us)

commit v2 on v1

v2 whole, which is shorter than its diff:
```python
import numpy as np

import jax
import jax.numpy as jnp
from jax import lax
from jax.experimental import pallas as pl
from jax.experimental.pallas import tpu as pltpu
from jax.sharding import PartitionSpec as P

STEPS = 2


CURRENT_GAIN = 0.08
WIND_GAIN = 0.06
DECAY_GAIN = 0.03
NONLINEAR_GAIN = 0.3
THERMAL = 0.2
HALINE = 0.8
CORIOLIS = 0.1
PRESSURE_GAIN = 0.2
LATERAL_MIX = 0.1
VERTICAL_MIX = 0.2
ADVECTION = 0.3
STRESS_GAIN = 150.0


def from_lower(block, axis):
    count = lax.axis_size(axis)
    return lax.ppermute(block, axis, [(i, i + 1) for i in range(count - 1)])


def from_upper(block, axis):
    count = lax.axis_size(axis)
    return lax.ppermute(block, axis, [(i + 1, i) for i in range(count - 1)])


def tables(total, directions):
    index = np.arange(total, dtype=np.float64)
    group = 0.4 * np.exp(-3.0 * index / (total - 1))
    ratio = np.exp(2.0 * index / (total - 1) - 1.0)
    angles = 2.0 * np.pi * np.arange(directions) / directions
    cosines, sines = np.cos(angles), np.sin(angles)
    full = np.zeros((total, directions, 8))
    full[..., 0] = group[:, None] * cosines
    full[..., 1] = group[:, None] * sines
    full[..., 2] = cosines
    full[..., 3] = sines
    full[..., 4] = 4.0 * group[:, None]
    full[..., 5] = ratio[:, None]
    return full.reshape(total * directions, 8).astype(np.float32)


VMEM_LIMIT = 56 * 1024 * 1024
CHUNK = 48


def dot_0(left, right):
    return lax.dot_general(
        left, right, (((0,), (0,)), ((), ())), preferred_element_type=jnp.float32
    )


def step_kernel(
    first, spectra, second, table, currents, wind, mask,
    state, pushes, push_from,
    prop, prop_16, other_16, ends, ends_t, beside, rows_out, rows_in, sums, other_sums,
    push_out, push_in, hidden, transfer, partial, side_send, side_recv, chunk_send, chunk_recv,
    sum_send, sum_recv, push_send, push_recv,
):
    comps, rows, cols = state.shape
    f32, b16 = jnp.float32, jnp.bfloat16
    chunks = comps // CHUNK
    me = lax.axis_index("comp")
    places = []
    for axis in ("gy", "gx"):
        at, count = lax.axis_index(axis), lax.axis_size(axis)
        places.append((axis, lax.rem(at + 1, count), at < count - 1))
        places.append((axis, lax.rem(at + count - 1, count), at > 0))
    beside[...] = jnp.zeros_like(beside)
    rows_in[...] = jnp.zeros_like(rows_in)
    push_in[...] = jnp.zeros_like(push_in)
    pushes[...] = jnp.zeros_like(pushes)
    ends[...] = jnp.zeros_like(ends)

    mesh_ids = pl.DeviceIdType.MESH
    barrier = pltpu.get_barrier_semaphore()
    for axis, place, there in places:
        @pl.when(there)
        def _(axis=axis, place=place):
            pl.semaphore_signal(barrier, inc=1, device_id={axis: place}, device_id_type=mesh_ids)
    pl.semaphore_signal(barrier, inc=1, device_id={"comp": 1 - me}, device_id_type=mesh_ids)

    def fill(i, carry):
        part = pl.ds(pl.multiple_of(i * CHUNK, CHUNK), CHUNK)
        for r in range(rows):
            line = spectra[part, r, :]
            state[part, r, :] = line
            ends[part, r : r + 1] = line[:, :1]
            ends[part, rows + r : rows + r + 1] = line[:, cols - 1 :]
            if r == 0:
                rows_out[0, 1, part, :] = line.astype(b16)
            if r == rows - 1:
                rows_out[0, 0, part, :] = line.astype(b16)
        return carry

    lax.fori_loop(0, chunks, fill, 0)
    pl.semaphore_wait(barrier, 1 + sum(jnp.where(there, 1, 0) for _, _, there in places))

    def remote(source, target, send, recv, where):
        return pltpu.make_async_remote_copy(
            src_ref=source, dst_ref=target, send_sem=send, recv_sem=recv,
            device_id=where, device_id_type=mesh_ids,
        )

    def side(s, n):
        axis, place, _ = places[n]
        if n < 2:
            source, target = rows_out.at[s, n], rows_in.at[s, n]
        else:
            source, target = ends_t.at[s, pl.ds(0, 8)], beside.at[s, n - 2, pl.ds(0, 8)]
        return remote(source, target, side_send.at[s, n], side_recv.at[s, n], {axis: place})

    def chunk(s, i):
        part = pl.ds(pl.multiple_of(i * CHUNK, CHUNK), CHUNK)
        return remote(
            prop_16.at[s, part], other_16.at[s, part],
            chunk_send.at[s, i], chunk_recv.at[s, i], {"comp": 1 - me},
        )

    def sum_copy(s):
        return remote(sums.at[s], other_sums.at[s], sum_send.at[s], sum_recv.at[s], {"comp": 1 - me})

    def push(n):
        axis, place, _ = places[n]
        return remote(push_out, push_in.at[n], push_send.at[n], push_recv.at[n], {axis: place})

    lane = lax.broadcasted_iota(jnp.int32, (CHUNK, cols), 1)

    def step(s, carry):
        ends_t[s] = ends[...].T
        for n in range(4):
            @pl.when(places[n][2])
            def _(n=n):
                side(s, n).start()
        for n in range(4):
            @pl.when(places[n ^ 1][2])
            def _(n=n):
                side(s, n).wait_recv()
        ends[...] = beside[s, 0].T
        partial[: ends.shape[0], :cols] = beside[s, 1].T

        def body(i, totals):
            part = pl.ds(pl.multiple_of(i * CHUNK, CHUNK), CHUNK)
            tab = table[part, :]
            gx, gy, cos, sin, phase, ratio = (
                jnp.broadcast_to(tab[:, n : n + 1], (CHUNK, cols)) for n in range(6)
            )
            near_w = ends[part, :]
            near_e = partial[part, :cols]
            lines = [rows_in[s, 0, part, :].astype(f32)]
            lines += [state[part, r, :] for r in range(rows)]
            lines += [rows_in[s, 1, part, :].astype(f32)]
            out = []
            for r in range(rows):
                here = lines[r + 1]
                before = jnp.where(
                    lane == 0, near_w[:, rows + r : rows + r + 1], pltpu.roll(here, 1, 1)
                )
                after = jnp.where(
                    lane == cols - 1, near_e[:, r : r + 1], pltpu.roll(here, cols - 1, 1)
                )
                cx = gx + CURRENT_GAIN * currents[0, r : r + 1, :]
                cy = gy + CURRENT_GAIN * currents[1, r : r + 1, :]
                flux = jnp.abs(cx) * (here - jnp.where(cx > 0.0, before, after))
                flux = flux + jnp.abs(cy) * (here - jnp.where(cy > 0.0, lines[r], lines[r + 2]))
                moved = mask[r : r + 1, :] * (here - flux)
                prop[r, part, :] = moved
                prop_16[s, part, r * cols : (r + 1) * cols] = moved.astype(b16)
                growth = WIND_GAIN * jnp.maximum(
                    wind[0, r : r + 1, :] * cos + wind[1, r : r + 1, :] * sin - phase, 0.0
                )
                pushed = growth * moved
                for value in (moved, ratio * moved, pushed * cos, pushed * sin):
                    out.append(value.reshape(CHUNK // 8, 8, cols).sum(axis=0))
            chunk(s, i).start()
            return tuple(t + o for t, o in zip(totals, out))

        zero = jnp.zeros((8, cols), f32)
        totals = lax.fori_loop(0, chunks, body, (zero,) * (4 * rows))
        for r in range(rows):
            for n in range(4):
                at = n * rows + r
                sums[s, at : at + 1, :] = totals[4 * r + n].sum(axis=0, keepdims=True)
        sum_copy(s).start()
        own = pl.multiple_of(me * comps, comps)
        partial[...] = dot_0(first[pl.ds(own, comps), :], prop_16[s])
        sum_copy(s).wait_recv()
        total = sums[s] + other_sums[s]
        pushes[...] += total[2 * rows :, :]

        @pl.when(s == STEPS - 1)
        def _():
            push_out[...] = pushes[...]
            for n in range(2):
                @pl.when(places[n][2])
                def _(n=n):
                    push(n).start()

        scale_up = 2.0 * comps
        floor = jnp.maximum(total[:rows, :], 1.0)
        spread_ratio = total[rows : 2 * rows, :] / floor
        squared = DECAY_GAIN * spread_ratio * spread_ratio
        gain = scale_up / floor
        back = NONLINEAR_GAIN * (floor / scale_up)

        def arrive(i, carry):
            chunk(s, i).wait_recv()
            return carry

        lax.fori_loop(0, chunks, arrive, 0)
        far_start = pl.multiple_of((1 - me) * comps, comps)
        pre = dot_0(first[pl.ds(far_start, comps), :], other_16[s]) + partial[...]
        pre = pre * jnp.concatenate([gain[r : r + 1, :] for r in range(rows)], axis=1)
        hidden[...] = (pre / (1.0 + jnp.exp(-pre))).astype(b16)
        transfer[...] = dot_0(second[...], hidden[...]).astype(b16)
        later = jnp.minimum(s + 1, STEPS - 1)

        for n in range(4):
            @pl.when(places[n][2])
            def _(n=n):
                side(s, n).wait_send()

        def update(i, carry):
            part = pl.ds(pl.multiple_of(i * CHUNK, CHUNK), CHUNK)
            tab = table[part, :]
            cos, sin, phase, ratio = (
                jnp.broadcast_to(tab[:, n : n + 1], (CHUNK, cols)) for n in range(2, 6)
            )
            for r in range(rows):
                growth = WIND_GAIN * jnp.maximum(
                    wind[0, r : r + 1, :] * cos + wind[1, r : r + 1, :] * sin - phase, 0.0
                )
                fresh = prop[r, part, :] * jnp.exp(growth - ratio * squared[r : r + 1, :])
                moved = transfer[part, r * cols : (r + 1) * cols].astype(f32)
                fresh = fresh + back[r : r + 1, :] * moved
                state[part, r, :] = fresh
                ends[part, r : r + 1] = fresh[:, :1]
                ends[part, rows + r : rows + r + 1] = fresh[:, cols - 1 :]
                if r == 0:
                    rows_out[later, 1, part, :] = fresh.astype(b16)
                if r == rows - 1:
                    rows_out[later, 0, part, :] = fresh.astype(b16)
            return carry

        lax.fori_loop(0, chunks, update, 0)

        def leave(i, carry):
            chunk(s, i).wait_send()
            return carry

        lax.fori_loop(0, chunks, leave, 0)
        sum_copy(s).wait_send()
        return carry

    lax.fori_loop(0, STEPS, step, 0)
    for n in range(2):
        @pl.when(places[n][2])
        def _(n=n):
            push(n).wait_send()

        @pl.when(places[n ^ 1][2])
        def _(n=n):
            push(n).wait_recv()
    push_from[...] = push_in[...]


def steps_call(first, state, second, table, currents, wind, mask):
    comps, rows, cols = state.shape
    units = first.shape[1]
    cells = rows * cols
    f32, b16 = jnp.float32, jnp.bfloat16
    wide = -(-comps // 128) * 128
    shape = jax.ShapeDtypeStruct
    dma = pltpu.SemaphoreType.DMA
    chunks = comps // CHUNK
    return pl.pallas_call(
        step_kernel,
        out_shape=(
            shape((comps, rows, cols), f32),
            shape((2 * rows, cols), f32),
            shape((2, 2 * rows, cols), f32),
        ),
        in_specs=[pl.BlockSpec(memory_space=pltpu.VMEM)] * 7,
        out_specs=(pl.BlockSpec(memory_space=pltpu.VMEM),) * 3,
        scratch_shapes=[
            pltpu.VMEM((rows, comps, cols), f32),
            pltpu.VMEM((STEPS, comps, cells), b16),
            pltpu.VMEM((STEPS, comps, cells), b16),
            pltpu.VMEM((wide, 128), f32),
            pltpu.VMEM((STEPS, 128, wide), f32),
            pltpu.VMEM((STEPS, 2, 128, wide), f32),
            pltpu.VMEM((STEPS, 2, comps, cols), b16),
            pltpu.VMEM((STEPS, 2, comps, cols), b16),
            pltpu.VMEM((STEPS, 4 * rows, cols), f32),
            pltpu.VMEM((STEPS, 4 * rows, cols), f32),
            pltpu.VMEM((2 * rows, cols), f32),
            pltpu.VMEM((2, 2 * rows, cols), f32),
            pltpu.VMEM((units, cells), b16),
            pltpu.VMEM((comps, cells), b16),
            pltpu.VMEM((units, cells), f32),
            dma((STEPS, 4)),
            dma((STEPS, 4)),
            dma((STEPS, chunks)),
            dma((STEPS, chunks)),
            dma((STEPS,)),
            dma((STEPS,)),
            dma((2,)),
            dma((2,)),
        ],
        compiler_params=pltpu.CompilerParams(
            vmem_limit_bytes=VMEM_LIMIT, collective_id=0, has_side_effects=True
        ),
        cost_estimate=pl.CostEstimate(
            flops=12 * comps * units * cells, bytes_accessed=24 * comps * cells, transcendentals=0
        ),
    )(first, state, second, table, currents, wind, mask)


def ocean_update(padded, stress, mask_f):

    def middle(field):
        return field[..., 1:-1, 1:-1]

    def eastern(field):
        return field[..., 1:-1, 2:]

    def western(field):
        return field[..., 1:-1, :-2]

    def northern(field):
        return field[..., 2:, 1:-1]

    def southern(field):
        return field[..., :-2, 1:-1]

    def spread(field):
        return (
            eastern(field)
            + western(field)
            + northern(field)
            + southern(field)
            - 4.0 * middle(field)
        )

    def column(field):
        upper_level = jnp.concatenate([field[:1], field[:-1]], axis=0)
        lower_level = jnp.concatenate([field[1:], field[-1:]], axis=0)
        return upper_level + lower_level - 2.0 * field

    density = -THERMAL * padded[2] + HALINE * padded[3]
    pressure = jnp.cumsum(density, axis=0) - 0.5 * density
    speed_u = middle(padded[0])
    speed_v = middle(padded[1])

    def carry_term(field):
        return speed_u * 0.5 * (eastern(field) - western(field)) + speed_v * 0.5 * (
            northern(field) - southern(field)
        )

    surface = (jnp.arange(padded.shape[1]) == 0).astype(jnp.float32)[:, None, None]
    tend_u = (
        CORIOLIS * speed_v
        - PRESSURE_GAIN * 0.5 * (eastern(pressure) - western(pressure))
        + LATERAL_MIX * spread(padded[0])
        + VERTICAL_MIX * column(speed_u)
        + STRESS_GAIN * surface * stress[0]
    )
    tend_v = (
        -CORIOLIS * speed_u
        - PRESSURE_GAIN * 0.5 * (northern(pressure) - southern(pressure))
        + LATERAL_MIX * spread(padded[1])
        + VERTICAL_MIX * column(speed_v)
        + STRESS_GAIN * surface * stress[1]
    )
    tend_t = (
        -ADVECTION * carry_term(padded[2])
        + LATERAL_MIX * spread(padded[2])
        + VERTICAL_MIX * column(middle(padded[2]))
    )
    tend_s = (
        -ADVECTION * carry_term(padded[3])
        + LATERAL_MIX * spread(padded[3])
        + VERTICAL_MIX * column(middle(padded[3]))
    )
    return middle(padded) + mask_f * jnp.stack([tend_u, tend_v, tend_t, tend_s])


def regrid(field, below, above, blocks, row_table):
    rows = field.shape[1]
    padded = jnp.concatenate([below, field, above], axis=1)
    first_row = lax.axis_index("gy") * rows
    offset = row_table[:, :, 0] - first_row - jnp.arange(rows)[:, None]
    offset = offset[None, :, :, None]
    selected = jnp.where(
        offset < 0,
        padded[:, :rows, None, :],
        jnp.where(offset == 0, padded[:, 1:-1, None, :], padded[:, 2:, None, :]),
    )
    return jnp.einsum("rbds,krbs->krd", blocks, selected, precision=lax.Precision.HIGHEST)


def local(
    spectra,
    wind_field,
    sea_mask,
    first_layer,
    second_layer,
    ocean_state,
    current_blocks,
    current_rows,
    stress_blocks,
    stress_rows,
):
    f32 = jnp.float32
    mask_f = sea_mask.astype(f32)
    rows, cols = sea_mask.shape
    half_freqs, directions = spectra.shape[:2]
    comps = half_freqs * directions
    total = 2 * comps
    me = lax.axis_index("comp")
    table = lax.dynamic_slice_in_dim(
        jnp.asarray(tables(2 * half_freqs, directions)), me * comps, comps, 0
    )
    ocean_low, ocean_high = ocean_state[:, :, :1], ocean_state[:, :, -1:]
    ocean_south = from_lower(ocean_high, "gy")
    ocean_north = from_upper(ocean_low, "gy")
    ocean_west = from_lower(ocean_state[..., -1], "gx")[..., None]
    ocean_east = from_upper(ocean_state[..., 0], "gx")[..., None]
    currents = regrid(
        ocean_state[:2, 0], ocean_south[:2, 0], ocean_north[:2, 0], current_blocks, current_rows
    )
    second_own = lax.dynamic_slice_in_dim(second_layer, me * comps, comps, 1)
    state, pushes, push_from = steps_call(
        first_layer,
        spectra.reshape(comps, rows, cols),
        second_own,
        table,
        currents,
        wind_field,
        mask_f,
    )
    whole = jnp.concatenate([pushes[None], push_from]) / (STEPS * total)
    whole = whole.reshape(3, 2, rows, cols)
    stress_ocean = regrid(
        whole[0], whole[1, :, -1:], whole[2, :, :1], stress_blocks, stress_rows
    )
    corner = jnp.zeros(ocean_west.shape[:2] + (1, 1), f32)
    padded = jnp.concatenate(
        [
            jnp.concatenate([corner, ocean_south, corner], axis=3),
            jnp.concatenate([ocean_west, ocean_state, ocean_east], axis=3),
            jnp.concatenate([corner, ocean_north, corner], axis=3),
        ],
        axis=2,
    )
    return (state.reshape(spectra.shape), ocean_update(padded, stress_ocean, mask_f))


def solution(mesh):
    placed = (
        P("comp", None, "gy", "gx"),
        P(None, "gy", "gx"),
        P("gy", "gx"),
        P(),
        P(),
        P(None, None, "gy", "gx"),
        P("gy", None, "gx", None),
        P("gy", None, "gx"),
        P("gy", None, "gx", None),
        P("gy", None, "gx"),
    )
    return jax.shard_map(
        local,
        mesh=mesh,
        in_specs=placed,
        out_specs=(P("comp", None, "gy", "gx"), P(None, None, "gy", "gx")),
        check_vma=False,
    )
```

time: 120 us -> 85.7 us (0.71)
  the two profiles are of different devices: /device:TPU:29 before, /device:TPU:0 now
where the time goes in v2:
time: 85.7 us; the launch traced here: 85.3 us
  Pallas kernels  58.8 us (69%)
  local copies, waits for them, and re-layouts  10.6 us (12%)
  starting transfers between devices  9.62 us (11%)
  other arithmetic  4.26 us (5%)
  matrix products  1.12 us (1%)
  between operations  0.91 us (1%)
    pallas_call x1, Pallas kernels, steps_call(): pl.pallas_call(step_kernel, out_shape=(shape((comps, rows, cols), f32), s...  58.8 us
    ppermute x2, starting transfers between devices, from_lower(): return lax.ppermute(block, axis, [(i, i + 1) for i in range(count - 1)])  7.03 us
    ppermute x2, starting transfers between devices, from_upper(): return lax.ppermute(block, axis, [(i + 1, i) for i in range(count - 1)])  2.59 us
  transfers between devices with their start and end apart: 4, of which 0 were waited for; matrix products, arithmetic and copies ran while one was open for 8% of the time, Pallas kernels for 0%

profile of v2, /device:TPU:0, one launch (start us, length us, event | category | flops | bytes accessed | tf_op | source)
XLA Modules:
  0.0 85.3 jit_solution(5415839439637411681)
XLA Ops:
  0.6 1.2 %fusion.64 = (f32[4,16,1,128]{3,2,1,0:T(1,128)S(1)}, f32[4,16,1,128]{3,2,1,0:T(1,128)S(1)}) fusion(f32[4,16,4,128]{3,2,1,0:T(4,128)} %param.16), kind=kLoop, calls=%fused_computation.102 | loop fusion | bytes 131072 | tf_op jit(solution)/shard_map/slice | solution.py:434
  1.8 1.3 %collective-permute-start.1 = (f32[4,16,1,128]{3,2,1,0:T(1,128)S(1)}, f32[4,16,1,128]{3,2,1,0:T(1,128)S(1)}, u32[]{:S(2)}, u32[]{:S(2)}) collective-permute-start(f32[4,16,1,128]{3,2,1,0:T(1,128)S(1)} %get-tuple-element.31), channel_id=1, source_target_pairs={{4,0},{8,4},{12,8},{5,1},{9,5},{13,9},{6,2},{10,6},{14,10},{7,3},{... | collective-permute-start | bytes 98312 | tf_op jit(solution)/shard_map/ppermute | solution.py:34
  3.1 5.6 %collective-permute-start = (f32[4,16,1,128]{3,2,1,0:T(1,128)S(1)}, f32[4,16,1,128]{3,2,1,0:T(1,128)S(1)}, u32[]{:S(2)}, u32[]{:S(2)}) collective-permute-start(f32[4,16,1,128]{3,2,1,0:T(1,128)S(1)} %get-tuple-element.30), channel_id=1, source_target_pairs={{0,4},{4,8},{8,12},{1,5},{5,9},{9,13},{2,6},{6,10},{10,14},{3,7},{... | collective-permute-start | bytes 98312 | tf_op jit(solution)/shard_map/ppermute | solution.py:29
  8.7 1.1 %fusion.63 = (f32[4,16,4,1]{3,2,1,0:T(4,128)S(1)}, f32[4,16,4,1]{3,2,1,0:T(4,128)S(1)}) fusion(f32[4,16,4,128]{3,2,1,0:T(4,128)} %param.16), kind=kLoop, calls=%fused_computation.101 | loop fusion | bytes 4096 | tf_op jit(solution)/shard_map/slice | solution.py:437
  9.8 0.2 copy.59
  10.0 1.5 %collective-permute-start.2 = (f32[4,16,4]{1,2,0:T(4,128)S(1)}, f32[4,16,4]{1,2,0:T(4,128)S(1)}, u32[]{:S(2)}, u32[]{:S(2)}) collective-permute-start(f32[4,16,4]{1,2,0:T(4,128)S(1)} %bitcast.77), channel_id=1, source_target_pairs={{0,1},{1,2},{2,3},{4,5},{5,6},{6,7},{8,9},{9,10},{10,11},{12,13},{... | collective-permute-start | bytes 3080 | tf_op jit(solution)/shard_map/ppermute | solution.py:29
  11.4 0.2 copy.60
  11.6 1.3 %collective-permute-start.3 = (f32[4,16,4]{1,2,0:T(4,128)S(1)}, f32[4,16,4]{1,2,0:T(4,128)S(1)}, u32[]{:S(2)}, u32[]{:S(2)}) collective-permute-start(f32[4,16,4]{1,2,0:T(4,128)S(1)} %bitcast.79), channel_id=1, source_target_pairs={{1,0},{2,1},{3,2},{5,4},{6,5},{7,6},{9,8},{10,9},{11,10},{13,12},{... | collective-permute-start | bytes 3080 | tf_op jit(solution)/shard_map/ppermute | solution.py:34
  12.9 0.7 slice_bitcast_fusion.4
  13.6 0.7 broadcast_subtract_fusion
  14.4 1.7 %constant_dynamic-slice_fusion.1.second = bf16[1024,576]{1,0:T(8,128)(2,1)} fusion(bf16[1024,1152]{1,0:T(8,128)(2,1)S(1)} %copy-done, s32[]{:T(128)S(6)} %select_n.18), kind=kLoop, calls=%fused_computation.90 | loop fusion | bytes 2359300 | tf_op jit(solution)/shard_map/dynamic_slice | solution.py:442
  16.0 0.7 constant_dynamic-slice_fusion.table
  17.0 0.6 convert_element_type.5.mask
  17.8 0.2 copy.61
  18.0 0.2 copy.62
  18.2 0.7 maximum_maximum_fusion
  18.9 0.1 fusion.55
  19.3 0.1 fusion.59
  19.5 0.4 copy-done.3
  19.9 0.6 convolution_bitcast_fusion.1
  20.5 0.6 copy.74
  21.1 58.8 %shard_map.122 = (f32[576,4,128]{2,1,0:T(4,128)}, f32[8,128]{1,0:T(8,128)}, f32[2,8,128]{2,1,0:T(8,128)}) custom-call(bf16[1152,1024]{1,0:T(8,128)(2,1)} %first.1, f32[576,4,128]{2,1,0:T(4,128)} %bitcast.86, bf16[1024,576]{1,0:T(8,128)(2,1)} %constant_dynamic-slice_fusion.1.second, f32[576,8]{1,0:T(8,128)} %constant_dynamic-slice_fusion.table, ...), custom_call_target="tpu_custom_call" | custom-call | flops 3623878656 | bytes 7077888 | tf_op jit(solution)/shard_map/pallas_call | solution.py:286
  79.9 0.8 copy.65
  80.7 0.7 copy.64
  81.4 0.7 fusion.42
  82.2 0.6 convolution_bitcast_fusion
  82.7 0.2 fusion.29
  82.9 0.2 fusion.33
  83.1 0.2 fusion.19
  83.3 0.2 fusion.11
  83.5 0.7 fusion
  84.2 1.0 %copy.76 = f32[16,36,4,128]{3,2,1,0:T(4,128)} copy(f32[16,36,4,128]{3,2,1,0:T(4,128)S(1)} %bitcast.69) | data formatting | bytes 2359296
  (44 shorter events, 0.9 us)
Async XLA Ops:
  0.6 13.7 %copy-start = (bf16[1024,1152]{1,0:T(8,128)(2,1)S(1)}, bf16[1024,1152]{1,0:T(8,128)(2,1)}, u32[]{:S(2)}) copy-start(bf16[1024,1152]{1,0:T(8,128)(2,1)} %param.15) | copy-start | bytes 7077892
  1.8 16.3 %collective-permute-start.1 = (f32[4,16,1,128]{3,2,1,0:T(1,128)S(1)}, f32[4,16,1,128]{3,2,1,0:T(1,128)S(1)}, u32[]{:S(2)}, u32[]{:S(2)}) collective-permute-start(f32[4,16,1,128]{3,2,1,0:T(1,128)S(1)} %get-tuple-element.31), channel_id=1, source_target_pairs={{4,0},{8,4},{12,8},{5,1},{9,5},{13,9},{6,2},{10,6},{14,10},{7,3},{... | collective-permute-start | bytes 98312 | tf_op jit(solution)/shard_map/ppermute | solution.py:34
  3.1 15.0 %collective-permute-start = (f32[4,16,1,128]{3,2,1,0:T(1,128)S(1)}, f32[4,16,1,128]{3,2,1,0:T(1,128)S(1)}, u32[]{:S(2)}, u32[]{:S(2)}) collective-permute-start(f32[4,16,1,128]{3,2,1,0:T(1,128)S(1)} %get-tuple-element.30), channel_id=1, source_target_pairs={{0,4},{4,8},{8,12},{1,5},{5,9},{9,13},{2,6},{6,10},{10,14},{3,7},{... | collective-permute-start | bytes 98312 | tf_op jit(solution)/shard_map/ppermute | solution.py:29
  10.0 7.8 %collective-permute-start.2 = (f32[4,16,4]{1,2,0:T(4,128)S(1)}, f32[4,16,4]{1,2,0:T(4,128)S(1)}, u32[]{:S(2)}, u32[]{:S(2)}) collective-permute-start(f32[4,16,4]{1,2,0:T(4,128)S(1)} %bitcast.77), channel_id=1, source_target_pairs={{0,1},{1,2},{2,3},{4,5},{5,6},{6,7},{8,9},{9,10},{10,11},{12,13},{... | collective-permute-start | bytes 3080 | tf_op jit(solution)/shard_map/ppermute | solution.py:29
  11.6 6.4 %collective-permute-start.3 = (f32[4,16,4]{1,2,0:T(4,128)S(1)}, f32[4,16,4]{1,2,0:T(4,128)S(1)}, u32[]{:S(2)}, u32[]{:S(2)}) collective-permute-start(f32[4,16,4]{1,2,0:T(4,128)S(1)} %bitcast.79), channel_id=1, source_target_pairs={{1,0},{2,1},{3,2},{5,4},{6,5},{7,6},{9,8},{10,9},{11,10},{13,12},{... | collective-permute-start | bytes 3080 | tf_op jit(solution)/shard_map/ppermute | solution.py:34
  14.3 1.7 %copy-start.5 = (f32[1152,8]{1,0:T(8,128)S(1)}, f32[1152,8]{1,0:T(8,128)}, u32[]{:S(2)}) copy-start(f32[1152,8]{1,0:T(8,128)} %constant.53.clone) | copy-start | bytes 110596
  14.3 2.7 %copy-start.7 = (s32[4,128]{1,0:T(4,128)S(1)}, s32[4,128]{1,0:T(4,128)}, u32[]{:S(2)}) copy-start(s32[4,128]{1,0:T(4,128)} %param.13) | copy-start | bytes 6148
  14.3 3.8 %copy-start.1 = (f32[4,16,4,128]{3,2,1,0:T(4,128)S(1)}, f32[4,16,4,128]{3,2,1,0:T(4,128)}, u32[]{:S(2)}) copy-start(f32[4,16,4,128]{3,2,1,0:T(4,128)} %param.16) | copy-start | bytes 393220
  18.9 1.0 %copy-start.3 = (f32[4,2,128,128]{3,2,1,0:T(8,128)S(1)}, f32[4,2,128,128]{3,2,1,0:T(8,128)}, u32[]{:S(2)}) copy-start(f32[4,2,128,128]{3,2,1,0:T(8,128)} %param.17) | copy-start | bytes 1572868
  21.1 61.1 %copy-start.4 = (f32[4,2,128,128]{3,2,1,0:T(8,128)S(1)}, f32[4,2,128,128]{3,2,1,0:T(8,128)}, u32[]{:S(2)}) copy-start(f32[4,2,128,128]{3,2,1,0:T(8,128)} %param.19) | copy-start | bytes 1572868
  79.9 3.6 %copy-start.6 = (f32[4,128]{1,0:T(4,128)S(1)}, f32[4,128]{1,0:T(4,128)}, u32[]{:S(2)}) copy-start(f32[4,128]{1,0:T(4,128)} %convert_element_type.5.mask) | copy-start | bytes 6148
  79.9 4.3 %copy-start.2 = (f32[576,4,128]{2,1,0:T(4,128)S(1)}, f32[576,4,128]{2,1,0:T(4,128)}, u32[]{:S(2)}) copy-start(f32[576,4,128]{2,1,0:T(4,128)} %get-tuple-element.5) | copy-start | bytes 3538948

commit v3 on v2

--- a/solution.py
+++ b/solution.py
@@ -22,16 +22,6 @@
 VERTICAL_MIX = 0.2
 ADVECTION = 0.3
 STRESS_GAIN = 150.0
-
-
-def from_lower(block, axis):
-    count = lax.axis_size(axis)
-    return lax.ppermute(block, axis, [(i, i + 1) for i in range(count - 1)])
-
-
-def from_upper(block, axis):
-    count = lax.axis_size(axis)
-    return lax.ppermute(block, axis, [(i + 1, i) for i in range(count - 1)])
 
 
 def tables(total, directions):
@@ -52,6 +42,7 @@
 
 VMEM_LIMIT = 56 * 1024 * 1024
 CHUNK = 48
+PIECES = 3
 
 
 def dot_0(left, right):
@@ -213,13 +204,17 @@
         gain = scale_up / floor
         back = NONLINEAR_GAIN * (floor / scale_up)
 
-        def arrive(i, carry):
-            chunk(s, i).wait_recv()
-            return carry
-
-        lax.fori_loop(0, chunks, arrive, 0)
         far_start = pl.multiple_of((1 - me) * comps, comps)
-        pre = dot_0(first[pl.ds(far_start, comps), :], other_16[s]) + partial[...]
+        group = chunks // PIECES
+        span = group * CHUNK
+        for g in range(PIECES):
+            for i in range(g * group, (g + 1) * group):
+                chunk(s, i).wait_recv()
+            at = pl.multiple_of(far_start + g * span, span)
+            pre = dot_0(first[pl.ds(at, span), :], other_16[s, g * span : (g + 1) * span, :])
+            pre = pre + partial[...]
+            if g < PIECES - 1:
+                partial[...] = pre
         pre = pre * jnp.concatenate([gain[r : r + 1, :] for r in range(rows)], axis=1)
         hidden[...] = (pre / (1.0 + jnp.exp(-pre))).astype(b16)
         transfer[...] = dot_0(second[...], hidden[...]).astype(b16)
@@ -326,6 +321,87 @@
     )(first, state, second, table, currents, wind, mask)
 
 
+def ocean_kernel(
+    state, south, north, west, east, low, high, ends, ends_t, rows_in, beside, send, recv
+):
+    count_all, rows, _ = state.shape
+    places = []
+    for axis in ("gy", "gx"):
+        at, count = lax.axis_index(axis), lax.axis_size(axis)
+        places.append((axis, lax.rem(at + 1, count), at < count - 1))
+        places.append((axis, lax.rem(at + count - 1, count), at > 0))
+    rows_in[...] = jnp.zeros_like(rows_in)
+    beside[...] = jnp.zeros_like(beside)
+    mesh_ids = pl.DeviceIdType.MESH
+    barrier = pltpu.get_barrier_semaphore()
+    for axis, place, there in places:
+        @pl.when(there)
+        def _(axis=axis, place=place):
+            pl.semaphore_signal(barrier, inc=1, device_id={axis: place}, device_id_type=mesh_ids)
+    ends[...] = jnp.zeros_like(ends)
+    low[...] = state[:, 0, :]
+    high[...] = state[:, rows - 1, :]
+    for r in range(rows):
+        line = state[:, r, :]
+        ends[:count_all, r : r + 1] = line[:, :1]
+        ends[:count_all, rows + r : rows + r + 1] = line[:, -1:]
+    ends_t[...] = ends[...].T
+    pl.semaphore_wait(barrier, sum(jnp.where(there, 1, 0) for _, _, there in places))
+
+    def side(n):
+        axis, place, _ = places[n]
+        if n < 2:
+            source, target = (high, low)[n], rows_in.at[n]
+        else:
+            source, target = ends_t.at[pl.ds(0, 8)], beside.at[n - 2, pl.ds(0, 8)]
+        return pltpu.make_async_remote_copy(
+            src_ref=source, dst_ref=target, send_sem=send.at[n], recv_sem=recv.at[n],
+            device_id={axis: place}, device_id_type=mesh_ids,
+        )
+
+    for n in range(4):
+        @pl.when(places[n][2])
+        def _(n=n):
+            side(n).start()
+    for n in range(4):
+        @pl.when(places[n ^ 1][2])
+        def _(n=n):
+            side(n).wait_recv()
+
+        @pl.when(places[n][2])
+        def _(n=n):
+            side(n).wait_send()
+    south[...] = rows_in[0]
+    north[...] = rows_in[1]
+    west[...] = beside[0].T[:count_all, rows : 2 * rows]
+    east[...] = beside[1].T[:count_all, :rows]
+
+
+def ocean_call(state):
+    count_all, rows, cols = state.shape
+    f32 = jnp.float32
+    wide = -(-count_all // 128) * 128
+    shape = jax.ShapeDtypeStruct
+    return pl.pallas_call(
+        ocean_kernel,
+        out_shape=(shape((count_all, cols), f32),) * 2 + (shape((count_all, rows), f32),) * 2,
+        in_specs=[pl.BlockSpec(memory_space=pltpu.VMEM)],
+        out_specs=(pl.BlockSpec(memory_space=pltpu.VMEM),) * 4,
+        scratch_shapes=[
+            pltpu.VMEM((count_all, cols), f32),
+            pltpu.VMEM((count_all, cols), f32),
+            pltpu.VMEM((wide, 128), f32),
+            pltpu.VMEM((128, wide), f32),
+            pltpu.VMEM((2, count_all, cols), f32),
+            pltpu.VMEM((2, 128, wide), f32),
+            pltpu.SemaphoreType.DMA((4,)),
+            pltpu.SemaphoreType.DMA((4,)),
+        ],
+        compiler_params=pltpu.CompilerParams(collective_id=1, has_side_effects=True),
+        cost_estimate=pl.CostEstimate(flops=100000, bytes_accessed=400000, transcendentals=0),
+    )(state)
+
+
 def ocean_update(padded, stress, mask_f):
 
     def middle(field):
@@ -431,11 +507,12 @@
     table = lax.dynamic_slice_in_dim(
         jnp.asarray(tables(2 * half_freqs, directions)), me * comps, comps, 0
     )
-    ocean_low, ocean_high = ocean_state[:, :, :1], ocean_state[:, :, -1:]
-    ocean_south = from_lower(ocean_high, "gy")
-    ocean_north = from_upper(ocean_low, "gy")
-    ocean_west = from_lower(ocean_state[..., -1], "gx")[..., None]
-    ocean_east = from_upper(ocean_state[..., 0], "gx")[..., None]
+    levels = ocean_state.shape[1]
+    south, north, west, east = ocean_call(ocean_state.reshape(4 * levels, rows, cols))
+    ocean_south = south.reshape(4, levels, 1, cols)
+    ocean_north = north.reshape(4, levels, 1, cols)
+    ocean_west = west.reshape(4, levels, rows, 1)
+    ocean_east = east.reshape(4, levels, rows, 1)
     currents = regrid(
         ocean_state[:2, 0], ocean_south[:2, 0], ocean_north[:2, 0], current_blocks, current_rows
     )

time: 85.7 us -> 81.6 us (0.952)
  starting transfers between devices: 9.62 us -> 0 us
  Pallas kernels: 58.8 us -> 65.2 us
  local copies, waits for them, and re-layouts: 10.6 us -> 8.81 us
  matrix products: 1.12 us -> 2.16 us
    ppermute x4 -> x0, starting transfers between devices: 9.62 us -> none  [the longest x2 7.03 us: from_lower(): return lax.ppermute(block, axis, [(i, i + 1) for i in range(count - 1)])]
    pallas_call x0 -> x1, Pallas kernels: none -> 8.46 us  [ocean_call(): pl.pallas_call(ocean_kernel, out_shape=(shape((count_all, cols), f32),) *...]
    slice x4 -> x0, local copies, waits for them, and re-layouts: 2.6 us -> none  [the longest x2 1.26 us: local(): ocean_west = from_lower(ocean_state[..., -1], 'gx')[..., None]]
    pallas_call x1, Pallas kernels: 58.8 us -> 56.7 us  [steps_call(): pl.pallas_call(step_kernel, out_shape=(shape((comps, rows, cols), f32), s...]
    dot_general x2, matrix products: 1.12 us -> 2.16 us  [regrid(): jnp.einsum('rbds,krbs->krd', blocks, selected, precision=lax.Precision.HI...]
    reshape x0 -> x2, local copies, waits for them, and re-layouts: none -> 1 us  [the longest x1 0.5 us: local(): ocean_west = west.reshape(4, levels, rows, 1)]
  transfers between devices with their start and end apart: 4 -> 0, of which waited for: 0 -> 0; matrix products, arithmetic and copies ran while one was open for 8% -> 0% of each run, Pallas kernels for 0% -> 0%
where the time goes in v3:
time: 81.6 us; the launch traced here: 81.2 us
  Pallas kernels  65.2 us (80%)
  local copies, waits for them, and re-layouts  8.81 us (11%)
  other arithmetic  4.24 us (5%)
  matrix products  2.16 us (3%)
  between operations  0.87 us (1%)
    pallas_call x1, Pallas kernels, steps_call(): pl.pallas_call(step_kernel, out_shape=(shape((comps, rows, cols), f32), s...  56.7 us
    pallas_call x1, Pallas kernels, ocean_call(): pl.pallas_call(ocean_kernel, out_shape=(shape((count_all, cols), f32),) *...  8.46 us
    dot_general x2, matrix products, regrid(): jnp.einsum('rbds,krbs->krd', blocks, selected, precision=lax.Precision.HI...  2.16 us
    dynamic_slice x1, local copies, waits for them, and re-layouts, local(): second_own = lax.dynamic_slice_in_dim(second_layer, me * comps, comps, 1)  1.66 us

profile of v3, /device:TPU:0, one launch (start us, length us, event | category | flops | bytes accessed | tf_op | source)
XLA Modules:
  0.0 81.2 jit_solution(3301606840346559008)
XLA Ops:
  0.6 8.5 %shard_map.122 = (f32[64,128]{1,0:T(8,128)}, f32[64,128]{1,0:T(8,128)}, f32[64,4]{1,0:T(8,128)}, f32[64,4]{1,0:T(8,128)}) custom-call(f32[64,4,128]{2,1,0:T(4,128)} %bitcast.74), custom_call_target="tpu_custom_call" | custom-call | flops 100000 | bytes 400000 | tf_op jit(solution)/shard_map/pallas_call | solution.py:385
  9.1 0.7 slice_bitcast_fusion.5
  9.8 0.7 slice_bitcast_fusion.4
  10.6 0.7 broadcast_subtract_fusion
  11.3 0.1 copy.13
  11.4 0.1 copy.16
  11.5 1.6 %convolution_bitcast_fusion.1 = f32[4,2,128]{2,1,0:T(2,128)S(1)} fusion(f32[4,2,128,128]{3,2,1,0:T(8,128)} %param.17, pred[4,2]{1,0:T(4,128)(4,1)S(1)} %copy.16, pred[4,2]{1,0:T(4,128)(4,1)S(1)} %copy.13, f32[2,4,128]{2,0,1:T(2,128)S(1)} %copy.19, f32[2,4,128]{2,0,1:T(2,128)S(1)} %copy.17, f32[2,4,128]{2,0,1:T(2,128)S(1)} %copy.15), kind=kOutput, calls=%fused_computation.2 | convolution fusion | flops 3149824 | bytes 540688 | tf_op jit(solution)/shard_map/rbds,krbs->krd/dot_general | solution.py:485
  13.1 0.6 copy.38
  13.7 1.7 %constant_dynamic-slice_fusion.1.second = bf16[1024,576]{1,0:T(8,128)(2,1)} fusion(bf16[1024,1152]{1,0:T(8,128)(2,1)S(1)} %copy-done, s32[]{:T(128)S(6)} %select_n.18), kind=kLoop, calls=%fused_computation.90 | loop fusion | bytes 2359300 | tf_op jit(solution)/shard_map/dynamic_slice | solution.py:519
  15.4 0.7 constant_dynamic-slice_fusion.table
  16.1 0.6 convert_element_type.5.mask
  16.7 56.7 %shard_map.123 = (f32[576,4,128]{2,1,0:T(4,128)}, f32[8,128]{1,0:T(8,128)}, f32[2,8,128]{2,1,0:T(8,128)}) custom-call(bf16[1152,1024]{1,0:T(8,128)(2,1)} %first.1, f32[576,4,128]{2,1,0:T(4,128)} %bitcast.94, bf16[1024,576]{1,0:T(8,128)(2,1)} %constant_dynamic-slice_fusion.1.second, f32[576,8]{1,0:T(8,128)} %constant_dynamic-slice_fusion.table, ...), custom_call_target="tpu_custom_call" | custom-call | flops 3623878656 | bytes 7077888 | tf_op jit(solution)/shard_map/pallas_call | solution.py:281
  73.4 0.7 copy.27
  74.1 0.7 copy.26
  74.8 0.7 fusion.42
  75.6 0.1 copy.25
  75.7 0.1 copy.30
  75.8 0.6 convolution_bitcast_fusion
  76.4 0.5 copy.22
  76.9 0.5 copy.23
  77.5 0.7 maximum_maximum_fusion
  78.2 0.1 fusion.55
  78.3 0.1 fusion.56
  78.4 0.1 reduce-window_subtract_fusion
  78.5 0.2 fusion.19
  78.7 0.2 fusion.11
  78.9 0.1 fusion.59
  79.1 0.1 fusion.60
  79.1 0.2 fusion.29
  79.3 0.2 fusion.33
  79.5 0.7 fusion
  80.2 1.0 %copy.40 = f32[16,36,4,128]{3,2,1,0:T(4,128)} copy(f32[16,36,4,128]{3,2,1,0:T(4,128)S(1)} %bitcast.75) | data formatting | bytes 2359296
  (38 shorter events, 0.2 us)
Async XLA Ops:
  0.6 13.1 %copy-start = (bf16[1024,1152]{1,0:T(8,128)(2,1)S(1)}, bf16[1024,1152]{1,0:T(8,128)(2,1)}, u32[]{:S(2)}) copy-start(bf16[1024,1152]{1,0:T(8,128)(2,1)} %param.15) | copy-start | bytes 7077892
  13.7 1.7 %copy-start.4 = (f32[1152,8]{1,0:T(8,128)S(1)}, f32[1152,8]{1,0:T(8,128)}, u32[]{:S(2)}) copy-start(f32[1152,8]{1,0:T(8,128)} %constant.53.clone) | copy-start | bytes 110596
  13.7 2.4 %copy-start.10 = (s32[4,128]{1,0:T(4,128)S(1)}, s32[4,128]{1,0:T(4,128)}, u32[]{:S(2)}) copy-start(s32[4,128]{1,0:T(4,128)} %param.13) | copy-start | bytes 6148
  16.7 59.1 %copy-start.3 = (f32[4,2,128,128]{3,2,1,0:T(8,128)S(1)}, f32[4,2,128,128]{3,2,1,0:T(8,128)}, u32[]{:S(2)}) copy-start(f32[4,2,128,128]{3,2,1,0:T(8,128)} %param.19) | copy-start | bytes 1572868
  16.7 59.7 %copy-start.8 = (f32[64,4]{1,0:T(8,128)S(1)}, f32[64,4]{1,0:T(8,128)}, u32[]{:S(2)}) copy-start(f32[64,4]{1,0:T(8,128)} %get-tuple-element.12) | copy-start | bytes 3076
  16.7 60.2 %copy-start.7 = (f32[64,4]{1,0:T(8,128)S(1)}, f32[64,4]{1,0:T(8,128)}, u32[]{:S(2)}) copy-start(f32[64,4]{1,0:T(8,128)} %get-tuple-element.13) | copy-start | bytes 3076
  16.7 60.7 %copy-start.1 = (f32[4,16,4,128]{3,2,1,0:T(4,128)S(1)}, f32[4,16,4,128]{3,2,1,0:T(4,128)}, u32[]{:S(2)}) copy-start(f32[4,16,4,128]{3,2,1,0:T(4,128)} %param.16) | copy-start | bytes 393220
  16.7 60.7 %copy-start.5 = (f32[64,128]{1,0:T(8,128)S(1)}, f32[64,128]{1,0:T(8,128)}, u32[]{:S(2)}) copy-start(f32[64,128]{1,0:T(8,128)} %get-tuple-element.9) | copy-start | bytes 98308
  16.7 60.7 %copy-start.6 = (f32[64,128]{1,0:T(8,128)S(1)}, f32[64,128]{1,0:T(8,128)}, u32[]{:S(2)}) copy-start(f32[64,128]{1,0:T(8,128)} %get-tuple-element.10) | copy-start | bytes 98308
  78.2 1.3 %copy-start.9 = (f32[4,128]{1,0:T(4,128)S(1)}, f32[4,128]{1,0:T(4,128)}, u32[]{:S(2)}) copy-start(f32[4,128]{1,0:T(4,128)} %convert_element_type.5.mask) | copy-start | bytes 6148
  78.4 1.8 %copy-start.2 = (f32[576,4,128]{2,1,0:T(4,128)S(1)}, f32[576,4,128]{2,1,0:T(4,128)}, u32[]{:S(2)}) copy-start(f32[576,4,128]{2,1,0:T(4,128)} %get-tuple-element.11) | copy-start | bytes 3538948

commit v4 on v3

--- a/solution.py
+++ b/solution.py
@@ -142,7 +142,7 @@
 
         def body(i, totals):
             part = pl.ds(pl.multiple_of(i * CHUNK, CHUNK), CHUNK)
-            tab = table[part, :]
+            tab = table[pl.ds(pl.multiple_of(me * comps + i * CHUNK, CHUNK), CHUNK), :]
             gx, gy, cos, sin, phase, ratio = (
                 jnp.broadcast_to(tab[:, n : n + 1], (CHUNK, cols)) for n in range(6)
             )
@@ -164,7 +164,7 @@
                 cy = gy + CURRENT_GAIN * currents[1, r : r + 1, :]
                 flux = jnp.abs(cx) * (here - jnp.where(cx > 0.0, before, after))
                 flux = flux + jnp.abs(cy) * (here - jnp.where(cy > 0.0, lines[r], lines[r + 2]))
-                moved = mask[r : r + 1, :] * (here - flux)
+                moved = mask[r : r + 1, :].astype(f32) * (here - flux)
                 prop[r, part, :] = moved
                 prop_16[s, part, r * cols : (r + 1) * cols] = moved.astype(b16)
                 growth = WIND_GAIN * jnp.maximum(
@@ -227,7 +227,7 @@
 
         def update(i, carry):
             part = pl.ds(pl.multiple_of(i * CHUNK, CHUNK), CHUNK)
-            tab = table[part, :]
+            tab = table[pl.ds(pl.multiple_of(me * comps + i * CHUNK, CHUNK), CHUNK), :]
             cos, sin, phase, ratio = (
                 jnp.broadcast_to(tab[:, n : n + 1], (CHUNK, cols)) for n in range(2, 6)
             )
@@ -504,9 +504,7 @@
     comps = half_freqs * directions
     total = 2 * comps
     me = lax.axis_index("comp")
-    table = lax.dynamic_slice_in_dim(
-        jnp.asarray(tables(2 * half_freqs, directions)), me * comps, comps, 0
-    )
+    table = jnp.asarray(tables(2 * half_freqs, directions))
     levels = ocean_state.shape[1]
     south, north, west, east = ocean_call(ocean_state.reshape(4 * levels, rows, cols))
     ocean_south = south.reshape(4, levels, 1, cols)
@@ -524,7 +522,7 @@
         table,
         currents,
         wind_field,
-        mask_f,
+        sea_mask,
     )
     whole = jnp.concatenate([pushes[None], push_from]) / (STEPS * total)
     whole = whole.reshape(3, 2, rows, cols)

time: 81.6 us -> 80.4 us (0.985)
  no operation moved by 1% of the time
where the time goes in v4:
time: 80.4 us; the launch traced here: 80 us
  Pallas kernels  65.2 us (81%)
  local copies, waits for them, and re-layouts  8.07 us (10%)
  other arithmetic  3.66 us (5%)
  matrix products  2.16 us (3%)
  between operations  0.87 us (1%)
    pallas_call x1, Pallas kernels, steps_call(): pl.pallas_call(step_kernel, out_shape=(shape((comps, rows, cols), f32), s...  56.8 us
    pallas_call x1, Pallas kernels, ocean_call(): pl.pallas_call(ocean_kernel, out_shape=(shape((count_all, cols), f32),) *...  8.46 us
    dot_general x2, matrix products, regrid(): jnp.einsum('rbds,krbs->krd', blocks, selected, precision=lax.Precision.HI...  2.16 us
    dynamic_slice x1, local copies, waits for them, and re-layouts, local(): second_own = lax.dynamic_slice_in_dim(second_layer, me * comps, comps, 1)  1.67 us

profile of v4, /device:TPU:0, one launch (start us, length us, event | category | flops | bytes accessed | tf_op | source)
XLA Modules:
  0.0 80.0 jit_solution(12403752845584954397)
XLA Ops:
  0.6 0.0 copy-start
  0.6 8.5 %shard_map.122 = (f32[64,128]{1,0:T(8,128)}, f32[64,128]{1,0:T(8,128)}, f32[64,4]{1,0:T(8,128)}, f32[64,4]{1,0:T(8,128)}) custom-call(f32[64,4,128]{2,1,0:T(4,128)} %bitcast.74), custom_call_target="tpu_custom_call" | custom-call | flops 100000 | bytes 400000 | tf_op jit(solution)/shard_map/pallas_call | solution.py:385
  9.1 0.7 slice_bitcast_fusion.5
  9.8 0.7 slice_bitcast_fusion.4
  10.6 0.7 broadcast_subtract_fusion
  11.3 0.1 copy.13
  11.4 0.1 copy.16
  11.5 1.6 %convolution_bitcast_fusion.1 = f32[4,2,128]{2,1,0:T(2,128)S(1)} fusion(f32[4,2,128,128]{3,2,1,0:T(8,128)} %param.17, pred[4,2]{1,0:T(4,128)(4,1)S(1)} %copy.16, pred[4,2]{1,0:T(4,128)(4,1)S(1)} %copy.13, f32[2,4,128]{2,0,1:T(2,128)S(1)} %copy.19, f32[2,4,128]{2,0,1:T(2,128)S(1)} %copy.17, f32[2,4,128]{2,0,1:T(2,128)S(1)} %copy.15), kind=kOutput, calls=%fused_computation.2 | convolution fusion | flops 3149824 | bytes 540688 | tf_op jit(solution)/shard_map/rbds,krbs->krd/dot_general | solution.py:485
  13.1 0.6 copy.38
  13.7 1.7 %constant_dynamic-slice_fusion.second = bf16[1024,576]{1,0:T(8,128)(2,1)} fusion(bf16[1024,1152]{1,0:T(8,128)(2,1)S(1)} %copy-done, s32[]{:T(128)S(6)} %select_n.17), kind=kLoop, calls=%fused_computation.89 | loop fusion | bytes 2359300 | tf_op jit(solution)/shard_map/dynamic_slice | solution.py:517
  15.4 56.8 %shard_map.123 = (f32[576,4,128]{2,1,0:T(4,128)}, f32[8,128]{1,0:T(8,128)}, f32[2,8,128]{2,1,0:T(8,128)}) custom-call(bf16[1152,1024]{1,0:T(8,128)(2,1)} %first.1, f32[576,4,128]{2,1,0:T(4,128)} %bitcast.94, bf16[1024,576]{1,0:T(8,128)(2,1)} %constant_dynamic-slice_fusion.second, f32[1152,8]{1,0:T(8,128)} %constant.53.clone.table, f32[2,4,128]{2,1,0:T(4,128)} %bitcast.91, ...), custom_call_target="tpu_custom_call" | custom-call | flops 3623878656 | bytes 7077888 | tf_op jit(solution)/shard_map/pallas_call | solution.py:281
  72.2 0.7 copy.27
  72.9 0.7 copy.26
  73.6 0.7 fusion.42
  74.3 0.1 copy.25
  74.5 0.1 copy.30
  74.6 0.6 convolution_bitcast_fusion
  75.1 0.0 copy-done.7
  75.2 0.5 copy.22
  75.7 0.5 copy.23
  76.2 0.7 maximum_maximum_fusion
  77.0 0.1 fusion.55
  77.1 0.1 fusion.56
  77.2 0.1 reduce-window_subtract_fusion
  77.3 0.2 fusion.19
  77.5 0.2 fusion.11
  77.7 0.1 fusion.59
  77.8 0.1 fusion.60
  77.9 0.2 fusion.29
  78.1 0.2 fusion.33
  78.3 0.7 fusion
  79.0 1.0 %copy.40 = f32[16,36,4,128]{3,2,1,0:T(4,128)} copy(f32[16,36,4,128]{3,2,1,0:T(4,128)S(1)} %bitcast.75) | data formatting | bytes 2359296
  (33 shorter events, 0.2 us)
Async XLA Ops:
  0.6 13.1 %copy-start = (bf16[1024,1152]{1,0:T(8,128)(2,1)S(1)}, bf16[1024,1152]{1,0:T(8,128)(2,1)}, u32[]{:S(2)}) copy-start(bf16[1024,1152]{1,0:T(8,128)(2,1)} %param.15) | copy-start | bytes 7077892
  15.4 59.2 %copy-start.3 = (f32[4,2,128,128]{3,2,1,0:T(8,128)S(1)}, f32[4,2,128,128]{3,2,1,0:T(8,128)}, u32[]{:S(2)}) copy-start(f32[4,2,128,128]{3,2,1,0:T(8,128)} %param.19) | copy-start | bytes 1572868
  15.4 59.8 %copy-start.7 = (f32[64,4]{1,0:T(8,128)S(1)}, f32[64,4]{1,0:T(8,128)}, u32[]{:S(2)}) copy-start(f32[64,4]{1,0:T(8,128)} %get-tuple-element.12) | copy-start | bytes 3076
  15.4 60.3 %copy-start.6 = (f32[64,4]{1,0:T(8,128)S(1)}, f32[64,4]{1,0:T(8,128)}, u32[]{:S(2)}) copy-start(f32[64,4]{1,0:T(8,128)} %get-tuple-element.13) | copy-start | bytes 3076
  15.4 60.8 %copy-start.1 = (f32[4,16,4,128]{3,2,1,0:T(4,128)S(1)}, f32[4,16,4,128]{3,2,1,0:T(4,128)}, u32[]{:S(2)}) copy-start(f32[4,16,4,128]{3,2,1,0:T(4,128)} %param.16) | copy-start | bytes 393220
  15.4 60.8 %copy-start.4 = (f32[64,128]{1,0:T(8,128)S(1)}, f32[64,128]{1,0:T(8,128)}, u32[]{:S(2)}) copy-start(f32[64,128]{1,0:T(8,128)} %get-tuple-element.9) | copy-start | bytes 98308
  15.4 60.8 %copy-start.5 = (f32[64,128]{1,0:T(8,128)S(1)}, f32[64,128]{1,0:T(8,128)}, u32[]{:S(2)}) copy-start(f32[64,128]{1,0:T(8,128)} %get-tuple-element.10) | copy-start | bytes 98308
  76.9 1.3 %copy-start.8 = (s32[4,128]{1,0:T(4,128)S(1)}, s32[4,128]{1,0:T(4,128)}, u32[]{:S(2)}) copy-start(s32[4,128]{1,0:T(4,128)} %mask.1) | copy-start | bytes 6148
  77.2 1.8 %copy-start.2 = (f32[576,4,128]{2,1,0:T(4,128)S(1)}, f32[576,4,128]{2,1,0:T(4,128)}, u32[]{:S(2)}) copy-start(f32[576,4,128]{2,1,0:T(4,128)} %get-tuple-element.11) | copy-start | bytes 3538948
